TPU v7x, 32 devices: a whole 2x2x4 slice. The times are simulated.
32 devices in a mesh: blk: 8 (over z, x), head: 4 (over y, core).
Axes of the slice: x: 2, y: 2, z: 4, core: 2. Of those that a mesh axis runs over, the one named last changes fastest.
Arguments:
- tokens: bfloat16 [8, 2048, 1280], P(None, ('blk', 'head')), may hold values from -6 to 6
- attn_gain: float32 [1280], replicated, may hold values from 0.1 to 1.9
- ffn_gain: float32 [1280], replicated, may hold values from 0.1 to 1.9
- query_weight: bfloat16 [1280, 1280], P('blk', 'head'), may hold values from -0.15625 to 0.15625
- keyval_weight: bfloat16 [2, 1280, 320], P(None, 'blk', 'head'), may hold values from -0.15625 to 0.15625
- output_weight: bfloat16 [1280, 1280], P('blk', 'head'), may hold values from -0.625 to 0.625
- gateup_weight: bfloat16 [2, 1280, 3584], P(None, 'blk', 'head'), may hold values from -0.15625 to 0.15625
- down_weight: bfloat16 [3584, 1280], P('blk', 'head'), may hold values from -0.09375 to 0.09375
- query_down: bfloat16 [8, 1280, 16], replicated, may hold values from -0.15625 to 0.15625
- query_up: bfloat16 [8, 16, 1280], replicated, may hold values from -0.375 to 0.375
- keyval_down: bfloat16 [8, 2, 1280, 16], replicated, may hold values from -0.15625 to 0.15625
- keyval_up: bfloat16 [8, 2, 16, 320], replicated, may hold values from -0.375 to 0.375
- output_down: bfloat16 [8, 1280, 16], replicated, may hold values from -0.15625 to 0.15625
- output_up: bfloat16 [8, 16, 1280], replicated, may hold values from -1.5 to 1.5
- gateup_down: bfloat16 [8, 2, 1280, 16], replicated, may hold values from -0.15625 to 0.15625
- gateup_up: bfloat16 [8, 2, 16, 3584], replicated, may hold values from -0.375 to 0.375
- ffdown_down: bfloat16 [8, 3584, 16], replicated, may hold values from -0.09375 to 0.09375
- ffdown_up: bfloat16 [8, 16, 1280], replicated, may hold values from -0.375 to 0.375
- segment_ids: int32 [8, 2048], replicated, may hold values from 0 to 1, as said below
- real_mask: int32 [8, 2048], replicated, may hold values from 0 to 1, as said below
- adapter_index: int32 [8], replicated, may hold values from 0 to 7, each once
- out_grad: bfloat16 [8, 2048, 1280], P(None, ('blk', 'head')), may hold values from -6 to 6
Outputs:
- output: bfloat16 [8, 2048, 1280], P(None, ('blk', 'head'))
- input_grad: bfloat16 [8, 2048, 1280], P(None, ('blk', 'head'))
- grad_query_down: float32 [8, 1280, 16], replicated
- grad_query_up: float32 [8, 16, 1280], replicated
- grad_keyval_down: float32 [8, 2, 1280, 16], replicated
- grad_keyval_up: float32 [8, 2, 16, 320], replicated
- grad_output_down: float32 [8, 1280, 16], replicated
- grad_output_up: float32 [8, 16, 1280], replicated
- grad_gateup_down: float32 [8, 2, 1280, 16], replicated
- grad_gateup_up: float32 [8, 2, 16, 3584], replicated
- grad_ffdown_down: float32 [8, 3584, 16], replicated
- grad_ffdown_up: float32 [8, 16, 1280], replicated
Inputs may be any that keep to these rules, and one draw needn't show every extreme that they name: `segment_ids`: numbers never fall along a sequence and begin at 0 in each; in every draw one sequence is a single document and another reaches the largest number. `real_mask`: each sequence's padding, if any, is a run at its end shorter than 128 positions. `adapter_index`: each adapter serves exactly one sequence.
All inputs are finite; a program needn't handle non-finite values.
Results may differ from a plain program's by a relative error of at most 0.019.
Values may be sent and summed in bfloat16 or wider, within the bound.
A program may use at most 320 MiB of HBM per device.

v0:
```python
import math

import jax
import jax.numpy as jnp
import numpy as np
from jax import lax
from jax.sharding import PartitionSpec as P

HEADS = 20
KV_HEADS = 5
HEAD_DIM = 64
WINDOW = 1024


EPSILON = 1e-05
ROPE_BASE = 10000.0
ADAPTER_SCALE = 2.0
MASKED = -1e30


def passed_along(value, axis, steps):
    count = lax.axis_size(axis)
    initial, last = (max(0, -steps), min(count, count - steps))
    return lax.ppermute(value, axis, [(source, source + steps) for source in range(initial, last)])


def rms_scale(values, gain):
    return values * lax.rsqrt(jnp.mean(values * values, axis=-1, keepdims=True) + EPSILON) * gain


def rotate(values, positions, sign):
    half = values.shape[-1] // 2
    freqs = ROPE_BASE ** (-(jnp.arange(half, dtype=jnp.float32) * 2.0) / values.shape[-1])
    angles = positions.astype(jnp.float32)[:, None] * freqs[None, :]
    cosine = jnp.cos(angles)[:, None, :]
    sine = sign * jnp.sin(angles)[:, None, :]
    first = values[..., :half]
    second = values[..., half:]
    return jnp.concatenate(
        [first * cosine - second * sine, second * cosine + first * sine], axis=-1
    )


def gated(gate, upward):
    return jax.nn.silu(gate) * upward


def project(inputs, weight, down, up):
    lowered = jnp.einsum("sci,sir->scr", inputs, down, preferred_element_type=jnp.float32).astype(
        jnp.bfloat16
    )
    extra = ADAPTER_SCALE * jnp.einsum(
        "scr,sro->sco", lowered, up, preferred_element_type=jnp.float32
    )
    return (
        jnp.einsum("sci,io->sco", inputs, weight, preferred_element_type=jnp.float32) + extra,
        lowered,
    )


def project_back(inputs, lowered, grad_out, weight, down, up):
    grad_up = ADAPTER_SCALE * jnp.einsum(
        "scr,sco->sro", lowered, grad_out, preferred_element_type=jnp.float32
    )
    grad_low = (
        ADAPTER_SCALE * jnp.einsum("sco,sro->scr", grad_out, up, preferred_element_type=jnp.float32)
    ).astype(jnp.bfloat16)
    grad_down = jnp.einsum("sci,scr->sir", inputs, grad_low, preferred_element_type=jnp.float32)
    grad_in = jnp.einsum("sco,io->sci", grad_out, weight, preferred_element_type=jnp.float32)
    grad_in = grad_in + jnp.einsum(
        "scr,sir->sci", grad_low, down, preferred_element_type=jnp.float32
    )
    return (grad_in, grad_down, grad_up)


def on_device(
    tokens,
    attn_gain,
    ffn_gain,
    query_weight,
    keyval_weight,
    output_weight,
    gateup_weight,
    down_weight,
    query_down,
    query_up,
    keyval_down,
    keyval_up,
    output_down,
    output_up,
    gateup_down,
    gateup_up,
    ffdown_down,
    ffdown_up,
    segment_ids,
    real_mask,
    adapter_index,
    out_grad,
):
    seqs, per_device, width = tokens.shape
    groups = lax.axis_size("head")
    head_pos = lax.axis_index("head")
    blk_pos = lax.axis_index("blk")
    span = groups * per_device
    heads = HEADS
    head_dim = HEAD_DIM
    kv_heads = KV_HEADS
    local_heads = heads // groups
    share = heads // kv_heads
    reach = (WINDOW - 2) // span + 1
    scale = 1.0 / math.sqrt(head_dim)
    rows_a, rows_b, rows_c, rows_d, rows_e = (
        lax.all_gather(query_weight, "blk", axis=0, tiled=True),
        lax.all_gather(keyval_weight, "blk", axis=1, tiled=True),
        lax.all_gather(output_weight, "blk", axis=0, tiled=True),
        lax.all_gather(gateup_weight, "blk", axis=1, tiled=True),
        lax.all_gather(down_weight, "blk", axis=0, tiled=True),
    )
    w_query, w_keyval, w_output, w_gateup, w_down = (
        lax.all_gather(rows_a, "head", axis=1, tiled=True),
        lax.all_gather(rows_b, "head", axis=2, tiled=True),
        lax.all_gather(rows_c, "head", axis=1, tiled=True),
        lax.all_gather(rows_d, "head", axis=2, tiled=True),
        lax.all_gather(rows_e, "head", axis=1, tiled=True),
    )
    down_query = query_down[adapter_index]
    up_query = query_up[adapter_index]
    down_keyval = keyval_down[adapter_index]
    up_keyval = keyval_up[adapter_index]
    down_output = output_down[adapter_index]
    up_output = output_up[adapter_index]
    down_gateup = gateup_down[adapter_index]
    up_gateup = gateup_up[adapter_index]
    down_ffdown = ffdown_down[adapter_index]
    up_ffdown = ffdown_up[adapter_index]

    def first_norm(values):
        return rms_scale(values, attn_gain)

    def second_norm(values):
        return rms_scale(values, ffn_gain)

    flat = tokens.astype(jnp.float32)
    normed_full, first_norm_back = jax.vjp(first_norm, flat)
    normed = normed_full.astype(jnp.bfloat16)
    queries_pre, low_query = project(normed, w_query, down_query, up_query)
    keys_pre, low_key = project(normed, w_keyval[0], down_keyval[:, 0], up_keyval[:, 0])
    values_pre, low_value = project(normed, w_keyval[1], down_keyval[:, 1], up_keyval[:, 1])
    token_pos = (blk_pos * groups + head_pos) * per_device + jnp.arange(per_device, dtype=jnp.int32)
    queries = rotate(queries_pre.reshape(seqs, per_device, heads, head_dim), token_pos, 1.0).astype(
        jnp.bfloat16
    )
    keys = rotate(keys_pre.reshape(seqs, per_device, kv_heads, head_dim), token_pos, 1.0).astype(
        jnp.bfloat16
    )
    values = values_pre.reshape(seqs, per_device, kv_heads, head_dim).astype(jnp.bfloat16)
    owner = np.array(
        [
            [(group * local_heads + slot) // share for slot in range(local_heads)]
            for group in range(groups)
        ]
    )
    slot_of = jnp.arange(local_heads, dtype=jnp.int32)
    sender = jnp.asarray(
        (owner[:, :, None] == np.arange(kv_heads)[None, None, :]).astype(np.float32), jnp.bfloat16
    )
    spread = (slot_of[:, None] == jnp.arange(local_heads, dtype=jnp.int32)[None, :]).astype(
        jnp.bfloat16
    )
    pair = jnp.stack([keys, values], axis=3)
    outgoing = jnp.einsum(
        "sckxd,gmk->scgmxd", pair, sender, preferred_element_type=jnp.float32
    ).astype(jnp.bfloat16)
    outgoing = outgoing.reshape(seqs, per_device, groups, local_heads * 2 * head_dim)
    query_send = queries.reshape(seqs, per_device, groups, local_heads * head_dim)
    query_here, pair_here = (
        lax.all_to_all(query_send, "head", split_axis=2, concat_axis=1, tiled=True),
        lax.all_to_all(outgoing, "head", split_axis=2, concat_axis=1, tiled=True),
    )
    query_here = query_here.reshape(seqs, span, local_heads, head_dim)
    pair_here = pair_here.reshape(seqs, span, local_heads, 2, head_dim)
    received = [pair_here]
    moving = pair_here
    for hop in range(reach):
        moving = passed_along(moving, "blk", 1)
        received.append(moving)
    window_pairs = jnp.stack(received, axis=1)
    query_pos = blk_pos * span + jnp.arange(span, dtype=jnp.int32)
    key_pos = (blk_pos - jnp.arange(reach + 1, dtype=jnp.int32))[:, None] * span + jnp.arange(
        span, dtype=jnp.int32
    )[None, :]
    safe_pos = jnp.clip(key_pos, 0, segment_ids.shape[1] - 1)
    query_segment = lax.dynamic_slice_in_dim(segment_ids, blk_pos * span, span, 1)
    key_segment = segment_ids[:, safe_pos]
    key_real = real_mask[:, safe_pos]
    distance = query_pos[:, None, None] - key_pos[None]
    allowed = (key_pos[None] >= 0) & (distance >= 0) & (distance < WINDOW)
    allowed = allowed & (query_segment[:, :, None, None] == key_segment[:, None])
    allowed = allowed & ((key_real[:, None] == 1) | (distance[None] == 0))
    batch = 1
    target = max(1, 512 // span)
    for option in range(1, seqs + 1):
        if seqs % option == 0 and option <= target:
            batch = option
    count = seqs // batch

    def grouped(array):
        return array.reshape((count, batch) + array.shape[1:])

    def scores_of(query_part, pair_part, allowed_part):
        keys_wide = jnp.einsum(
            "gjlmd,hm->gjlhd", pair_part[:, :, :, :, 0], spread, preferred_element_type=jnp.float32
        ).astype(jnp.bfloat16)
        values_wide = jnp.einsum(
            "gjlmd,hm->gjlhd", pair_part[:, :, :, :, 1], spread, preferred_element_type=jnp.float32
        ).astype(jnp.bfloat16)
        raw = (
            jnp.einsum(
                "gqhd,gjlhd->ghqjl", query_part, keys_wide, preferred_element_type=jnp.float32
            )
            * scale
        )
        raw = jnp.where(allowed_part[:, None], raw, MASKED)
        return (raw, keys_wide, values_wide)

    def attend(pieces):
        query_part, pair_part, allowed_part = pieces
        raw, keys_wide, values_wide = scores_of(query_part, pair_part, allowed_part)
        top = jnp.max(raw, axis=(3, 4), keepdims=True)
        shifted = jnp.exp(raw - top)
        total = jnp.sum(shifted, axis=(3, 4), keepdims=True)
        probs_low = (shifted / total).astype(jnp.bfloat16)
        result = jnp.einsum(
            "ghqjl,gjlhd->gqhd", probs_low, values_wide, preferred_element_type=jnp.float32
        )
        return (result.astype(jnp.bfloat16), top + jnp.log(total))

    attended, logsum = lax.map(
        attend, (grouped(query_here), grouped(window_pairs), grouped(allowed))
    )
    mixed = lax.all_to_all(
        attended.reshape(seqs, span, local_heads * head_dim),
        "head",
        split_axis=1,
        concat_axis=2,
        tiled=True,
    )
    branch_attn, low_output = project(mixed, w_output, down_output, up_output)
    middle = flat + branch_attn
    normed2_full, second_norm_back = jax.vjp(second_norm, middle)
    normed2 = normed2_full.astype(jnp.bfloat16)
    gate, low_gate = project(normed2, w_gateup[0], down_gateup[:, 0], up_gateup[:, 0])
    upward, low_upward = project(normed2, w_gateup[1], down_gateup[:, 1], up_gateup[:, 1])
    activated_full, gated_back = jax.vjp(gated, gate, upward)
    activated = activated_full.astype(jnp.bfloat16)
    branch_ffn, low_ffdown = project(activated, w_down, down_ffdown, up_ffdown)
    output = (middle + branch_ffn).astype(jnp.bfloat16)
    grad_activated, gd_ffdown, gu_ffdown = project_back(
        activated, low_ffdown, out_grad, w_down, down_ffdown, up_ffdown
    )
    grad_gate, grad_upward = gated_back(grad_activated)
    grad_in_gate, gd_gate, gu_gate = project_back(
        normed2,
        low_gate,
        grad_gate.astype(jnp.bfloat16),
        w_gateup[0],
        down_gateup[:, 0],
        up_gateup[:, 0],
    )
    grad_in_up, gd_up, gu_up = project_back(
        normed2,
        low_upward,
        grad_upward.astype(jnp.bfloat16),
        w_gateup[1],
        down_gateup[:, 1],
        up_gateup[:, 1],
    )
    grad_middle = out_grad.astype(jnp.float32) + second_norm_back(grad_in_gate + grad_in_up)[0]
    grad_mixed, gd_output, gu_output = project_back(
        mixed, low_output, grad_middle.astype(jnp.bfloat16), w_output, down_output, up_output
    )
    grad_send = grad_mixed.astype(jnp.bfloat16).reshape(
        seqs, per_device, groups, local_heads * head_dim
    )
    grad_here = lax.all_to_all(grad_send, "head", split_axis=2, concat_axis=1, tiled=True).reshape(
        seqs, span, local_heads, head_dim
    )
    spread_full = spread.astype(jnp.float32)

    def attend_back(pieces):
        query_part, pair_part, allowed_part, logsum_part, grad_part = pieces
        raw, keys_wide, values_wide = scores_of(query_part, pair_part, allowed_part)
        probs = jnp.exp(raw - logsum_part)
        probs_low = probs.astype(jnp.bfloat16)
        grad_probs = jnp.einsum(
            "gqhd,gjlhd->ghqjl", grad_part, values_wide, preferred_element_type=jnp.float32
        )
        inner = jnp.sum(probs * grad_probs, axis=(3, 4), keepdims=True)
        grad_raw = (probs * (grad_probs - inner)).astype(jnp.bfloat16)
        grad_query = scale * jnp.einsum(
            "ghqjl,gjlhd->gqhd", grad_raw, keys_wide, preferred_element_type=jnp.float32
        )
        grad_keys = scale * jnp.einsum(
            "ghqjl,gqhd->gjlhd", grad_raw, query_part, preferred_element_type=jnp.float32
        )
        grad_values = jnp.einsum(
            "ghqjl,gqhd->gjlhd", probs_low, grad_part, preferred_element_type=jnp.float32
        )
        both = jnp.stack([grad_keys, grad_values], axis=4)
        folded = jnp.einsum("gjlhxd,hm->gjlmxd", both, spread_full, precision=lax.Precision.HIGHEST)
        return (grad_query, folded)

    grad_query, grad_pairs = lax.map(
        attend_back,
        (grouped(query_here), grouped(window_pairs), grouped(allowed), logsum, grouped(grad_here)),
    )
    grad_pairs = grad_pairs.reshape(seqs, reach + 1, span, local_heads, 2, head_dim)
    carried = grad_pairs[:, reach]
    for hop in range(reach - 1, -1, -1):
        carried = (
            passed_along(carried.astype(jnp.bfloat16), "blk", -1).astype(carried.dtype)
            + grad_pairs[:, hop]
        )
    grad_query = rotate(grad_query.reshape(seqs, span, local_heads, head_dim), query_pos, -1.0)
    grad_query = grad_query.astype(jnp.bfloat16).reshape(seqs, span, local_heads * head_dim)
    grad_queries_pre = lax.all_to_all(grad_query, "head", split_axis=1, concat_axis=2, tiled=True)
    grad_pair_tok = lax.all_to_all(
        carried.reshape(seqs, span, local_heads * 2 * head_dim).astype(jnp.bfloat16),
        "head",
        split_axis=1,
        concat_axis=2,
        tiled=True,
    ).astype(jnp.float32)
    grad_pair_tok = grad_pair_tok.reshape(seqs, per_device, groups, local_heads, 2, head_dim)
    grad_pair_heads = jnp.einsum(
        "scgmxd,gmk->sckxd",
        grad_pair_tok,
        sender.astype(jnp.float32),
        precision=lax.Precision.HIGHEST,
    )
    grad_keys_pre = (
        rotate(grad_pair_heads[:, :, :, 0], token_pos, -1.0)
        .astype(jnp.bfloat16)
        .reshape(seqs, per_device, kv_heads * head_dim)
    )
    grad_values_pre = (
        grad_pair_heads[:, :, :, 1]
        .astype(jnp.bfloat16)
        .reshape(seqs, per_device, kv_heads * head_dim)
    )
    grad_in_query, gd_query, gu_query = project_back(
        normed, low_query, grad_queries_pre, w_query, down_query, up_query
    )
    grad_in_key, gd_key, gu_key = project_back(
        normed, low_key, grad_keys_pre, w_keyval[0], down_keyval[:, 0], up_keyval[:, 0]
    )
    grad_in_value, gd_value, gu_value = project_back(
        normed, low_value, grad_values_pre, w_keyval[1], down_keyval[:, 1], up_keyval[:, 1]
    )
    grad_normed = grad_in_query + grad_in_key + grad_in_value
    input_grad = (grad_middle + first_norm_back(grad_normed)[0]).astype(jnp.bfloat16)
    chooser = (
        adapter_index[:, None] == jnp.arange(query_down.shape[0], dtype=jnp.int32)[None, :]
    ).astype(jnp.float32)

    def per_adapter(per_sequence):
        return jnp.einsum("sa,s...->a...", chooser, per_sequence, precision=lax.Precision.HIGHEST)

    sums = lax.psum(
        (
            per_adapter(gd_query),
            per_adapter(gu_query),
            per_adapter(jnp.stack([gd_key, gd_value], axis=1)),
            per_adapter(jnp.stack([gu_key, gu_value], axis=1)),
            per_adapter(gd_output),
            per_adapter(gu_output),
            per_adapter(jnp.stack([gd_gate, gd_up], axis=1)),
            per_adapter(jnp.stack([gu_gate, gu_up], axis=1)),
            per_adapter(gd_ffdown),
            per_adapter(gu_ffdown),
        ),
        ("blk", "head"),
    )
    return (
        output,
        input_grad,
        sums[0],
        sums[1],
        sums[2],
        sums[3],
        sums[4],
        sums[5],
        sums[6],
        sums[7],
        sums[8],
        sums[9],
    )


def solution(mesh):
    in_specs = (
        P(None, ("blk", "head"), None),
        P(),
        P(),
        P("blk", "head"),
        P(None, "blk", "head"),
        P("blk", "head"),
        P(None, "blk", "head"),
        P("blk", "head"),
        P(),
        P(),
        P(),
        P(),
        P(),
        P(),
        P(),
        P(),
        P(),
        P(),
        P(),
        P(),
        P(),
        P(None, ("blk", "head"), None),
    )
    out_specs = (
        P(None, ("blk", "head"), None),
        P(None, ("blk", "head"), None),
        P(),
        P(),
        P(),
        P(),
        P(),
        P(),
        P(),
        P(),
        P(),
        P(),
    )
    return jax.shard_map(
        on_device, mesh=mesh, in_specs=in_specs, out_specs=out_specs, check_vma=False
    )
```

profile of v0, /device:TPU:0, one launch (start us, length us, event | category | flops | bytes accessed | tf_op | source)
XLA Modules:
  0.0 1731.3 jit_solution(17322591747086908637)
XLA Ops:
  8.3 33.5 %all_gather.30 = bf16[2,1280,80]{2,0,1:T(2,128)(2,1)S(1)} all-gather(bf16[2,160,80]{2,0,1:T(2,128)(2,1)S(1)} %copy.338), channel_id=1, replica_groups=mesh['blk'=8,'head'=4] {'blk'}, dimensions={1}, use_global_device_ids=true | all-gather | bytes 460800 | tf_op jit(solution)/shard_map/all_gather | solution.py:114
  43.8 33.3 %all_gather.32 = bf16[1280,320]{1,0:T(8,128)(2,1)S(1)} all-gather(bf16[160,320]{1,0:T(8,128)(2,1)S(1)} %copy-done.89), channel_id=1, replica_groups=mesh['blk'=8,'head'=4] {'blk'}, dimensions={0}, use_global_device_ids=true | all-gather | bytes 921600 | tf_op jit(solution)/shard_map/all_gather | solution.py:113
  79.0 37.3 %all_gather.34 = bf16[1280,320]{1,0:T(8,128)(2,1)} all-gather(bf16[160,320]{1,0:T(8,128)(2,1)S(1)} %copy-done.90), channel_id=1, replica_groups=mesh['blk'=8,'head'=4] {'blk'}, dimensions={0}, use_global_device_ids=true | all-gather | bytes 921600 | tf_op jit(solution)/shard_map/all_gather | solution.py:115
  184.4 35.8 %all_to_all.96 = bf16[8,64,4,640]{3,1,0,2:T(8,128)(2,1)} all-to-all(bf16[8,64,4,640]{3,1,0,2:T(8,128)(2,1)} %reshape.607), channel_id=1, replica_groups=mesh['blk'=8,'head'=4] {'head'}, dimensions={2} | all-to-all | bytes 5242880 | tf_op jit(solution)/shard_map/all_to_all | solution.py:178
  242.6 54.8 %collective-permute-done = bf16[8,256,5,2,64]{1,4,3,2,0:T(8,128)(2,1)} collective-permute-done((bf16[8,256,5,2,64]{1,4,3,2,0:T(8,128)(2,1)}, bf16[8,256,5,2,64]{1,4,3,2,0:T(8,128)(2,1)}, u32[]{:S(2)}, u32[]{:S(2)}) %collective-permute-start) | collective-permute-done | bytes 2621472 | tf_op jit(solution)/shard_map/ppermute | solution.py:24
  324.2 33.1 %collective-permute-done.1 = bf16[8,256,5,2,64]{1,4,3,2,0:T(8,128)(2,1)} collective-permute-done((bf16[8,256,5,2,64]{1,4,3,2,0:T(8,128)(2,1)}, bf16[8,256,5,2,64]{1,4,3,2,0:T(8,128)(2,1)}, u32[]{:S(2)}, u32[]{:S(2)}) %collective-permute-start.1) | collective-permute-done | bytes 2621472 | tf_op jit(solution)/shard_map/ppermute | solution.py:24
  399.0 17.2 collective-permute-done.2
  477.5 11.8 copy.356
  518.6 11.4 copy.358
  538.4 51.1 %copy.367 = bf16[4,2,5,256,5,2,64]{3,6,5,4,2,1,0:T(8,128)(2,1)} copy(bf16[4,2,5,256,5,2,64]{6,5,4,3,1,0,2:T(2,128)(2,1)} %constant_dynamic-update-slice_fusion) | data formatting | bytes 26214400
  589.6 112.3 %while.28 = (s32[]{:T(128)}, bf16[4,2,256,5,64]{2,4,3,1,0:T(8,128)(2,1)}, f32[4,2,5,256,1,1]{3,2,1,5,4,0:T(8,128)}, bf16[4,2,5,256,5,2,64]{3,6,5,4,2,1,0:T(8,128...) while((s32[]{:T(128)}, ...), condition=%wide.region_4.5_spmd.clone.clone, body=%wide.region_1.4_spmd.clone.clone.sunk | while | flops 896366208 | bytes 67262560 | solution.py:238
  747.0 12.0 fusion.85
  821.4 60.2 %copy.379 = bf16[4,2,5,256,5,2,64]{3,4,6,2,1,5,0:T(8,128)(2,1)} copy(bf16[4,2,5,256,5,2,64]{6,5,4,3,1,0,2:T(2,128)(2,1)} %constant_dynamic-update-slice_fusion) | data formatting | bytes 26214400
  889.2 237.1 %while.29 = (s32[]{:T(128)}, f32[4,2,256,5,64]{2,4,3,1,0:T(8,128)}, f32[4,2,5,256,5,2,64]{3,6,5,4,1,0,2:T(8,128)}, bf16[4,2,5,256,5,2,64]{3,4,6,2,1,5,0:T(8,128)...) while((s32[]{:T(128)}, f32[4,2,256,5,64]{2,4,3,1,0:T(8,128)}, ...), condition=%wide.region_9.10_spmd.clone.clone, body=%wide.region_7.9_spmd.clone.clone.sunk | while | flops 2265249280 | bytes 206188816 | solution.py:313
  929.9 13.8 fusion.343
  989.0 13.8 fusion.343
  1048.1 13.8 fusion.343
  1107.2 13.8 fusion.343
  1130.5 60.1 %collective-permute-done.4 = bf16[8,256,5,2,64]{1,4,3,2,0:T(8,128)(2,1)S(1)} collective-permute-done((bf16[8,256,5,2,64]{1,4,3,2,0:T(8,128)(2,1)S(1)}, bf16[8,256,5,2,64]{1,4,3,2,0:T(8,128)(2,1)S(1)}, u32[]{:S(2)}, u32[]{:S(2)}) %collective-permute-start.4) | collective-permute-done | bytes 2621472 | tf_op jit(solution)/shard_map/ppermute | solution.py:24
  1195.6 59.9 %collective-permute-done.5 = bf16[8,256,5,2,64]{1,4,3,2,0:T(8,128)(2,1)S(1)} collective-permute-done((bf16[8,256,5,2,64]{1,4,3,2,0:T(8,128)(2,1)S(1)}, bf16[8,256,5,2,64]{1,4,3,2,0:T(8,128)(2,1)S(1)}, u32[]{:S(2)}, u32[]{:S(2)}) %collective-permute-start.5) | collective-permute-done | bytes 2621472 | tf_op jit(solution)/shard_map/ppermute | solution.py:24
  1267.0 52.6 %collective-permute-done.6 = bf16[8,256,5,2,64]{1,4,3,2,0:T(8,128)(2,1)S(1)} collective-permute-done((bf16[8,256,5,2,64]{1,4,3,2,0:T(8,128)(2,1)S(1)}, bf16[8,256,5,2,64]{1,4,3,2,0:T(8,128)(2,1)S(1)}, u32[]{:S(2)}, u32[]{:S(2)}) %collective-permute-start.6) | collective-permute-done | bytes 2621472 | tf_op jit(solution)/shard_map/ppermute | solution.py:24
  1348.0 36.6 %collective-permute-done.7 = bf16[8,256,5,2,64]{1,4,3,2,0:T(8,128)(2,1)} collective-permute-done((bf16[8,256,5,2,64]{1,4,3,2,0:T(8,128)(2,1)}, bf16[8,256,5,2,64]{1,4,3,2,0:T(8,128)(2,1)}, u32[]{:S(2)}, u32[]{:S(2)}) %collective-permute-start.7) | collective-permute-done | bytes 2621472 | tf_op jit(solution)/shard_map/ppermute | solution.py:24
  1419.6 11.8 all-to-all-done.5
  1491.5 215.1 %all-reduce.3.cloned.1.call-done = (f32[8,1280,16]{1,0,2:T(8,128)}, f32[8,16,1280]{2,0,1:T(8,128)}, f32[8,2,1280,16]{2,0,3,1:T(8,128)}, f32[8,2,16,320]{3,0,2,1:...) async-done(((f32[8,1280,16]{1,0,2:T(8,128)}, ...) | async-done | bytes 11730960 | tf_op jit(solution)/shard_map/psum | solution.py:369
  (573 shorter events, 831.1 us)
Async XLA Ops:
  7.2 705.8 %copy-start = (bf16[8,2,16,3584]{3,2,1,0:T(8,128)(2,1)S(1)}, bf16[8,2,16,3584]{3,2,1,0:T(8,128)(2,1)}, u32[]{:S(2)}) copy-start(bf16[8,2,16,3584]{3,2,1,0:T(8,128)(2,1)} %param.42) | copy-start | bytes 5505028
  7.2 120.4 %all-gather.9.cloned.1.call-start = ((), (), s32[]{:S(2)}) async-start(), calls=%async_computation.6 | async-start | bytes 2048000 | tf_op jit(solution)/shard_map/all_gather | solution.py:121
  43.0 88.0 %all-gather.21.cloned.1.call-start = ((), (), s32[]{:S(2)}) async-start(), calls=%async_computation.12 | async-start | bytes 2949120 | tf_op jit(solution)/shard_map/all_gather | solution.py:117
  43.7 324.6 %all-gather.11.cloned.1.call-start = ((), (), s32[]{:S(2)}) async-start(), calls=%async_computation.7 | async-start | bytes 4096000 | tf_op jit(solution)/shard_map/all_gather | solution.py:120
  78.4 399.1 %all-gather.15.cloned.1.call-start = ((), (), s32[]{:S(2)}) async-start(), calls=%async_computation.9 | async-start | bytes 5160960 | tf_op jit(solution)/shard_map/all_gather | solution.py:116
  79.0 660.4 %all-gather.13.cloned.1.call-start = ((), (), s32[]{:S(2)}) async-start(), calls=%async_computation.8 | async-start | bytes 4096000 | tf_op jit(solution)/shard_map/all_gather | solution.py:122
  118.5 628.5 %all-gather.19.cloned.1.call-start = ((), (), s32[]{:S(2)}) async-start(), calls=%async_computation.11 | async-start | bytes 11468800 | tf_op jit(solution)/shard_map/all_gather | solution.py:124
  124.0 255.9 %copy-start.62 = (f32[64,32]{1,0:T(8,128)}, f32[64,32]{1,0:T(8,128)S(1)}, u32[]{:S(2)}) copy-start(f32[64,32]{1,0:T(8,128)S(1)} %get-tuple-element.373) | copy-start | bytes 24580
  228.6 83.5 %copy-start.92 = (s32[8,2048]{1,0:T(8,128)S(1)}, s32[8,2048]{1,0:T(8,128)}, u32[]{:S(2)}) copy-start(s32[8,2048]{1,0:T(8,128)} %param.46) | copy-start | bytes 196612
  237.0 60.3 %collective-permute-start = (bf16[8,256,5,2,64]{1,4,3,2,0:T(8,128)(2,1)}, bf16[8,256,5,2,64]{1,4,3,2,0:T(8,128)(2,1)}, u32[]{:S(2)}, u32[]{:S(2)}) collective-permute-start(bf16[8,256,5,2,64]{1,4,3,2,0:T(8,128)(2,1)} %reshape.608), channel_id=1, source_target_pairs={{0,4},{4,8},{8,12},{12,16},{16,20},{20,24},{24,28},{1,5},{5,9},{9,... | collective-permute-start | bytes 7864328 | tf_op jit(solution)/shard_map/ppermute | solution.py:24
  297.4 59.9 %collective-permute-start.1 = (bf16[8,256,5,2,64]{1,4,3,2,0:T(8,128)(2,1)}, bf16[8,256,5,2,64]{1,4,3,2,0:T(8,128)(2,1)}, u32[]{:S(2)}, u32[]{:S(2)}) collective-permute-start(bf16[8,256,5,2,64]{1,4,3,2,0:T(8,128)(2,1)} %collective-permute-done), channel_id=1, source_target_pairs={{0,4},{4,8},{8,12},{12,16},{16,20},{20,24},{24,28},{1,5},{5,9},{9,... | collective-permute-start | bytes 7864328 | tf_op jit(solution)/shard_map/ppermute | solution.py:24
  357.2 58.9 %collective-permute-start.2 = (bf16[8,256,5,2,64]{1,4,3,2,0:T(8,128)(2,1)}, bf16[8,256,5,2,64]{1,4,3,2,0:T(8,128)(2,1)}, u32[]{:S(2)}, u32[]{:S(2)}) collective-permute-start(bf16[8,256,5,2,64]{1,4,3,2,0:T(8,128)(2,1)} %collective-permute-done.1), channel_id=1, source_target_pairs={{0,4},{4,8},{8,12},{12,16},{16,20},{20,24},{24,28},{1,5},{5,9},{9,... | collective-permute-start | bytes 7864328 | tf_op jit(solution)/shard_map/ppermute | solution.py:24
  395.4 54.8 %all-to-all-start.1 = ((bf16[8,64,4,320]{3,1,0,2:T(8,128)(2,1)}), bf16[8,64,4,320]{3,1,0,2:T(8,128)(2,1)S(1)}, u32[]{:S(2)}, u32[]{:S(2)}) async-start(bf16[8,64,4,320]{3,1,0,2:T(8,128)(2,1)} %copy.365), calls=%async_computation.1 | async-start | bytes 3145728 | tf_op jit(solution)/shard_map/all_to_all | solution.py:177
  399.0 360.0 %all-gather.17.cloned.1.call-start = ((), (), s32[]{:S(2)}) async-start(), calls=%async_computation.10 | async-start | bytes 22937600 | tf_op jit(solution)/shard_map/all_gather | solution.py:123
  416.2 102.4 %collective-permute-start.3 = (bf16[8,256,5,2,64]{1,4,3,2,0:T(8,128)(2,1)}, bf16[8,256,5,2,64]{1,4,3,2,0:T(8,128)(2,1)}, u32[]{:S(2)}, u32[]{:S(2)}) collective-permute-start(bf16[8,256,5,2,64]{1,4,3,2,0:T(8,128)(2,1)} %collective-permute-done.2), channel_id=1, source_target_pairs={{0,4},{4,8},{8,12},{12,16},{16,20},{20,24},{24,28},{1,5},{5,9},{9,... | collective-permute-start | bytes 7864328 | tf_op jit(solution)/shard_map/ppermute | solution.py:24
  705.2 24.7 %all-to-all-start.2 = ((bf16[8,256,320]{2,0,1:T(8,128)(2,1)}), bf16[8,256,320]{2,0,1:T(8,128)(2,1)}, u32[]{:S(2)}, u32[]{:S(2)}) async-start(bf16[8,256,320]{2,0,1:T(8,128)(2,1)} %copy.368), calls=%async_computation.2 | async-start | bytes 3145728 | tf_op jit(solution)/shard_map/all_to_all | solution.py:241
  817.8 63.8 %all-to-all-start.3 = ((bf16[8,64,4,320]{3,1,0,2:T(8,128)(2,1)}), bf16[8,64,4,320]{3,1,0,2:T(8,128)(2,1)S(1)}, u32[]{:S(2)}, u32[]{:S(2)}) async-start(bf16[8,64,4,320]{3,1,0,2:T(8,128)(2,1)} %copy.377), calls=%async_computation.3 | async-start | bytes 3145728 | tf_op jit(solution)/shard_map/all_to_all | solution.py:285
  1129.2 61.4 %collective-permute-start.4 = (bf16[8,256,5,2,64]{1,4,3,2,0:T(8,128)(2,1)S(1)}, bf16[8,256,5,2,64]{1,4,3,2,0:T(8,128)(2,1)S(1)}, u32[]{:S(2)}, u32[]{:S(2)}) collective-permute-start(bf16[8,256,5,2,64]{1,4,3,2,0:T(8,128)(2,1)S(1)} %fusion.137), channel_id=1, source_target_pairs={{4,0},{8,4},{12,8},{16,12},{20,16},{24,20},{28,24},{5,1},{9,5},{13... | collective-permute-start | bytes 7864328 | tf_op jit(solution)/shard_map/ppermute | solution.py:24
  1194.2 61.4 %collective-permute-start.5 = (bf16[8,256,5,2,64]{1,4,3,2,0:T(8,128)(2,1)S(1)}, bf16[8,256,5,2,64]{1,4,3,2,0:T(8,128)(2,1)S(1)}, u32[]{:S(2)}, u32[]{:S(2)}) collective-permute-start(bf16[8,256,5,2,64]{1,4,3,2,0:T(8,128)(2,1)S(1)} %fusion.106), channel_id=1, source_target_pairs={{4,0},{8,4},{12,8},{16,12},{20,16},{24,20},{28,24},{5,1},{9,5},{13... | collective-permute-start | bytes 7864328 | tf_op jit(solution)/shard_map/ppermute | solution.py:24
  1259.1 60.5 %collective-permute-start.6 = (bf16[8,256,5,2,64]{1,4,3,2,0:T(8,128)(2,1)S(1)}, bf16[8,256,5,2,64]{1,4,3,2,0:T(8,128)(2,1)S(1)}, u32[]{:S(2)}, u32[]{:S(2)}) collective-permute-start(bf16[8,256,5,2,64]{1,4,3,2,0:T(8,128)(2,1)S(1)} %fusion.104), channel_id=1, source_target_pairs={{4,0},{8,4},{12,8},{16,12},{20,16},{24,20},{28,24},{5,1},{9,5},{13... | collective-permute-start | bytes 7864328 | tf_op jit(solution)/shard_map/ppermute | solution.py:24
  1324.6 60.0 %collective-permute-start.7 = (bf16[8,256,5,2,64]{1,4,3,2,0:T(8,128)(2,1)}, bf16[8,256,5,2,64]{1,4,3,2,0:T(8,128)(2,1)}, u32[]{:S(2)}, u32[]{:S(2)}) collective-permute-start(bf16[8,256,5,2,64]{1,4,3,2,0:T(8,128)(2,1)} %fusion.102), channel_id=1, source_target_pairs={{4,0},{8,4},{12,8},{16,12},{20,16},{24,20},{28,24},{5,1},{9,5},{13... | collective-permute-start | bytes 7864328 | tf_op jit(solution)/shard_map/ppermute | solution.py:24
  1340.7 54.6 %all-to-all-start.4 = ((bf16[8,256,320]{2,0,1:T(8,128)(2,1)}), bf16[8,256,320]{2,0,1:T(8,128)(2,1)S(1)}, u32[]{:S(2)}, u32[]{:S(2)}) async-start(bf16[8,256,320]{2,0,1:T(8,128)(2,1)} %copy.380), calls=%async_computation.4 | async-start | bytes 3145728 | tf_op jit(solution)/shard_map/all_to_all | solution.py:326
  1395.3 36.1 %all-to-all-start.5 = ((bf16[8,256,640]{2,0,1:T(8,128)(2,1)}), bf16[8,256,640]{2,0,1:T(8,128)(2,1)}, u32[]{:S(2)}, u32[]{:S(2)}) async-start(bf16[8,256,640]{2,0,1:T(8,128)(2,1)} %copy.384), calls=%async_computation.5 | async-start | bytes 5242880 | tf_op jit(solution)/shard_map/all_to_all | solution.py:327
  1400.0 306.6 %all-reduce.3.cloned.1.call-start = ((), (), s32[]{:S(2)}) async-start(), calls=%async_computation.13 | async-start | bytes 23592960 | tf_op jit(solution)/shard_map/psum | solution.py:369
  (125 other events, 1323.8 us)
Sparse Core Ops, SparseCore 0:
  43.1 21.0 all-gather.8
  66.3 62.1 all-gather.20
  130.7 28.5 all-gather.10
  161.3 78.2 all-gather.14
  241.6 27.4 all-gather.12
  270.5 62.7 all-gather.18
  477.6 115.2 all-gather.16
  1469.1 237.5 all-reduce.2
where the time goes:
time: 1750 us; the launch traced here: 1730 us
  waiting for transfers between devices  553 us (32%)
  local copies, waits for them, and re-layouts  469 us (27%)
  matrix products  385 us (22%)
  blocking collectives  140 us (8%)
  other arithmetic  117 us (7%)
  starting transfers between devices  49.6 us (3%)
    ppermute x8, waiting for transfers between devices, passed_along(): lax.ppermute(value, axis, [(source, source + steps) for source in range(i...  314 us
    psum x1, waiting for transfers between devices, on_device(): lax.psum((per_adapter(gd_query), per_adapter(gu_query), per_adapter(jnp.s...  215 us
    unnamed x238, local copies, waits for them, and re-layouts  190 us
    another operation x6, local copies, waits for them, and re-layouts, on_device(): window_pairs = jnp.stack(received, axis=1)  64 us
    dot_general x4, matrix products, attend_back(): jnp.einsum('gjlhxd,hm->gjlmxd', both, spread_full, precision=lax.Precisio...  55.3 us
    dot_general x7, matrix products, project(): jnp.einsum('sci,io->sco', inputs, weight, preferred_element_type=jnp.floa...  39.4 us
    dot_general x4, matrix products, attend_back(): jnp.einsum('gqhd,gjlhd->ghqjl', grad_part, values_wide, preferred_element...  38.8 us
    all_gather x1, blocking collectives, on_device(): lax.all_gather(output_weight, 'blk', axis=0, tiled=True)  37.3 us
  transfers between devices with their start and end apart: 21, of which 10 were waited for; matrix products, arithmetic and copies ran while one was open for 34% of the time, Pallas kernels for 0%

commit v1 on v0

--- a/solution.py
+++ b/solution.py
@@ -1,9 +1,12 @@
+import functools
 import math
 
 import jax
 import jax.numpy as jnp
 import numpy as np
 from jax import lax
+from jax.experimental import pallas as pl
+from jax.experimental.pallas import tpu as pltpu
 from jax.sharding import PartitionSpec as P
 
 HEADS = 20
@@ -397,6 +400,734 @@
     )
 
 
+MESH = pl.DeviceIdType.MESH
+F32 = jnp.float32
+BF16 = jnp.bfloat16
+TILE = 128
+ANYWHERE = pl.BlockSpec(memory_space=pl.ANY)
+
+
+def dot(left, right, left_dim=1, right_dim=0):
+    return lax.dot_general(
+        left, right, (((left_dim,), (right_dim,)), ((), ())), preferred_element_type=F32
+    )
+
+
+def place():
+    blk, head = lax.axis_index("blk"), lax.axis_index("head")
+    return blk // 2, blk % 2, head // 2, head % 2
+
+
+def device(z, x, y, core):
+    return (z * 2 + x, y * 2 + core)
+
+
+def halves(count):
+    first = (count // 2 + 15) // 16 * 16
+    return ((0, first), (first, count - first))
+
+
+class Spread:
+    def __init__(self, sources, target, lines, sems):
+        self.sources, self.target, self.lines = sources, target, lines
+        self.z, self.x, self.y, self.core = place()
+        self.z_in, self.x_in, self.y_in, self.d_in, self.c_in = sems[:5]
+        self.z_out, self.x_out, self.y_out, self.d_out, self.c_out = sems[5:10]
+
+    @staticmethod
+    def semaphores(parts, lines):
+        dma = pltpu.SemaphoreType.DMA
+        return [
+            dma((parts, lines)),
+            dma((parts, lines)),
+            dma((parts, lines)),
+            dma((parts, lines, 2)),
+            dma((parts, lines, 4)),
+            dma((parts, 2, lines)),
+            dma((parts, lines)),
+            dma((parts, lines)),
+            dma((parts, lines, 2)),
+            dma((parts, lines, 4)),
+        ]
+
+    def inside(self, z):
+        return (z >= 0) & (z < self.lines)
+
+    def neighbours(self):
+        z, x, y, core = self.z, self.x, self.y, self.core
+        return (device(z, 1 - x, y, core), device(z, x, 1 - y, core), device(z, x, y, 1 - core))
+
+    def greet(self):
+        barrier = pltpu.get_barrier_semaphore()
+        for side in (1, -1):
+
+            @pl.when(self.inside(self.z + side))
+            def _():
+                other = device(self.z + side, self.x, self.y, self.core)
+                pl.semaphore_signal(barrier, inc=1, device_id=other, device_id_type=MESH)
+
+        for other in self.neighbours():
+            pl.semaphore_signal(barrier, inc=1, device_id=other, device_id_type=MESH)
+        ends = jnp.where(self.z > 0, 1, 0) + jnp.where(self.z < self.lines - 1, 1, 0)
+        pl.semaphore_wait(barrier, 3 + ends)
+
+    def copy(self, source, target, out, into, other):
+        return pltpu.make_async_remote_copy(
+            src_ref=source,
+            dst_ref=target,
+            send_sem=out,
+            recv_sem=into,
+            device_id=other,
+            device_id_type=MESH,
+        )
+
+    def along_z(self, part, source, z, side):
+        return self.copy(
+            source,
+            self.target(part, z, self.x, self.y, self.core),
+            self.z_out.at[part, (side + 1) // 2, z],
+            self.z_in.at[part, z],
+            device(self.z + side, self.x, self.y, self.core),
+        )
+
+    def along_x(self, part, source, z):
+        return self.copy(
+            source,
+            self.target(part, z, self.x, self.y, self.core),
+            self.x_out.at[part, z],
+            self.x_in.at[part, z],
+            device(self.z, 1 - self.x, self.y, self.core),
+        )
+
+    def along_y(self, part, source, z):
+        return self.copy(
+            source,
+            self.target(part, z, self.x, self.y, self.core),
+            self.y_out.at[part, z],
+            self.y_in.at[part, z],
+            device(self.z, self.x, 1 - self.y, self.core),
+        )
+
+    def across(self, part, source, z, flip_x, flip_y):
+        x, y = (self.x + flip_x) % 2, (self.y + flip_y) % 2
+        return self.copy(
+            source,
+            self.target(part, z, x, y, self.core),
+            self.c_out.at[part, z, flip_x * 2 + flip_y],
+            self.c_in.at[part, z, flip_x * 2 + flip_y],
+            device(self.z, self.x, self.y, 1 - self.core),
+        )
+
+    def piece(self, ref, which):
+        begin, size = halves(ref.shape[0])[which]
+        return ref.at[pl.ds(begin, size)]
+
+    def diagonal(self, part, z, which):
+        if which == 0:
+            ref = self.target(part, z, self.x, 1 - self.y, self.core)
+            other = device(self.z, 1 - self.x, self.y, self.core)
+        else:
+            ref = self.target(part, z, 1 - self.x, self.y, self.core)
+            other = device(self.z, self.x, 1 - self.y, self.core)
+        ref = self.piece(ref, which)
+        return self.copy(
+            ref, ref, self.d_out.at[part, z, which], self.d_in.at[part, z, which], other
+        )
+
+    def arrived(self, ref, out, into):
+        self.copy(ref, ref, out, into, device(self.z, self.x, self.y, 1 - self.core)).wait_recv()
+
+    def hand_on(self, part, source, z):
+        self.along_x(part, source, z).start()
+        self.along_y(part, source, z).start()
+        self.across(part, source, z, 0, 0).start()
+
+    def begin(self, part):
+        for side in (1, -1):
+
+            @pl.when(self.inside(self.z + side))
+            def _():
+                self.along_z(part, self.sources[part], self.z, side).start()
+
+        self.hand_on(part, self.sources[part], self.z)
+
+    def line_step(self, part, distance, side):
+        z = self.z - side * distance
+
+        @pl.when(self.inside(z))
+        def _():
+            ref = self.target(part, z, self.x, self.y, self.core)
+            self.arrived(ref, self.z_out.at[part, 0, z], self.z_in.at[part, z])
+
+            @pl.when(self.inside(self.z + side))
+            def _():
+                self.along_z(part, ref, z, side).start()
+
+            self.hand_on(part, ref, z)
+
+    def plane_step(self, part, z):
+        ref = self.target(part, z, self.x, 1 - self.y, self.core)
+        self.arrived(ref, self.y_out.at[part, z], self.y_in.at[part, z])
+        self.diagonal(part, z, 0).start()
+        self.across(part, ref, z, 0, 1).start()
+        ref = self.target(part, z, 1 - self.x, self.y, self.core)
+        self.arrived(ref, self.x_out.at[part, z], self.x_in.at[part, z])
+        self.diagonal(part, z, 1).start()
+        self.across(part, ref, z, 1, 0).start()
+
+    def corner_step(self, part, z):
+        ref = self.target(part, z, 1 - self.x, 1 - self.y, self.core)
+        for which in (0, 1):
+            self.arrived(
+                self.piece(ref, which), self.d_out.at[part, z, which], self.d_in.at[part, z, which]
+            )
+        self.across(part, ref, z, 1, 1).start()
+
+    def end(self, part, z):
+        for flip_x in (0, 1):
+            for flip_y in (0, 1):
+                x, y = (self.x + flip_x) % 2, (self.y + flip_y) % 2
+                which = flip_x * 2 + flip_y
+                self.arrived(
+                    self.target(part, z, x, y, 1 - self.core),
+                    self.c_out.at[part, z, which],
+                    self.c_in.at[part, z, which],
+                )
+                self.across(
+                    part, self.target(part, z, x, y, self.core), z, flip_x, flip_y
+                ).wait_send()
+        mine = self.target(part, z, self.x, self.y, self.core)
+        self.along_x(part, mine, z).wait_send()
+        self.along_y(part, mine, z).wait_send()
+        self.diagonal(part, z, 0).wait_send()
+        self.diagonal(part, z, 1).wait_send()
+        for side in (1, -1):
+
+            @pl.when(self.inside(self.z + side) & ((self.z - z) * side >= 0))
+            def _():
+                self.along_z(part, mine, z, side).wait_send()
+
+    def all_steps(self, parts):
+        for part in parts:
+            for distance in range(1, self.lines):
+                for side in (1, -1):
+                    self.line_step(part, distance, side)
+        for part in parts:
+            for z in range(self.lines):
+                self.plane_step(part, z)
+        for part in parts:
+            for z in range(self.lines):
+                self.corner_step(part, z)
+        for part in parts:
+            for z in range(self.lines):
+                self.end(part, z)
+
+
+def paired(own, other, core):
+    own, other = own.astype(F32), other.astype(F32)
+    return [jnp.where(core == 0, own, other), jnp.where(core == 0, other, own)]
+
+
+def gather_kernel(lines, *refs):
+    query, keyval, output, gateup, down, w_qkv, w_output, w_gateup, w_down = refs[:9]
+    got_query, got_keyval, got_output, got_down, my_qkv, my_output, my_down = refs[9:16]
+    pair_out, pair_in, local = refs[16:19]
+    rows, deep = my_qkv.shape[0], my_down.shape[0]
+    wide, mixed = my_output.shape[1], my_qkv.shape[1]
+    span, hidden = gateup.shape[1:]
+
+    def target(part, z, x, y, core):
+        blk, head = z * 2 + x, y * 2 + core
+        if part == 0:
+            return w_qkv.at[pl.ds(blk * 2 * rows + core * rows, rows), pl.ds(y * mixed, mixed)]
+        if part == 1:
+            return w_output.at[pl.ds(blk * 2 * rows + core * rows, rows), pl.ds(y * wide, wide)]
+        if part == 4:
+            return w_down.at[pl.ds(blk * 2 * deep + core * deep, deep), pl.ds(y * wide, wide)]
+        return w_gateup.at[part - 2, pl.ds(blk * span, span), pl.ds(head * hidden, hidden)]
+
+    sources = [my_qkv, my_output, gateup.at[0], gateup.at[1], my_down]
+    spread = Spread(sources, target, lines, refs[19:])
+    core = spread.core
+    spread.greet()
+    sibling = device(spread.z, spread.x, spread.y, 1 - core)
+    theirs = pl.ds((1 - core) * rows, rows)
+    swaps = [
+        spread.copy(query.at[theirs], got_query, pair_out.at[0], pair_in.at[0], sibling),
+        spread.copy(keyval.at[:, theirs], got_keyval, pair_out.at[1], pair_in.at[1], sibling),
+        spread.copy(output.at[theirs], got_output, pair_out.at[2], pair_in.at[2], sibling),
+        spread.copy(
+            down.at[pl.ds((1 - core) * deep, deep)], got_down, pair_out.at[3], pair_in.at[3], sibling
+        ),
+    ]
+    for swap in swaps:
+        swap.start()
+    mine = pl.ds(core * rows, rows)
+    swaps[0].wait_recv()
+    swaps[1].wait_recv()
+    pieces = paired(query[mine, :], got_query[...], core)
+    pieces += paired(keyval[0, mine, :], got_keyval[0], core)
+    pieces += paired(keyval[1, mine, :], got_keyval[1], core)
+    filled = sum(p.shape[1] for p in pieces)
+    pieces.append(jnp.zeros((rows, mixed - filled), F32))
+    my_qkv[...] = jnp.concatenate(pieces, axis=1).astype(BF16)
+    spread.begin(0)
+    swaps[2].wait_recv()
+    my_output[...] = jnp.concatenate(
+        paired(output[mine, :], got_output[...], core), axis=1
+    ).astype(BF16)
+    spread.begin(1)
+    spread.begin(2)
+    spread.begin(3)
+    swaps[3].wait_recv()
+    my_down[...] = jnp.concatenate(
+        paired(down[pl.ds(core * deep, deep), :], got_down[...], core), axis=1
+    ).astype(BF16)
+    spread.begin(4)
+    own = [
+        pltpu.make_async_copy(
+            sources[part],
+            target(part, spread.z, spread.x, spread.y, core),
+            local.at[part],
+        )
+        for part in range(5)
+    ]
+    for copy in own:
+        copy.start()
+    spread.all_steps(range(5))
+    for copy in own:
+        copy.wait()
+    for swap in swaps:
+        swap.wait_send()
+
+
+def gather_weights(query, keyval, output, gateup, down):
+    rows, wide = query.shape
+    deep = down.shape[0]
+    blks, heads = lax.axis_size("blk"), lax.axis_size("head")
+    narrow = keyval.shape[2]
+    mixed = -(-2 * (wide + 2 * narrow) // TILE) * TILE
+    dma = pltpu.SemaphoreType.DMA
+    vmem = pl.BlockSpec(memory_space=pltpu.VMEM)
+    shape = jax.ShapeDtypeStruct
+    return pl.pallas_call(
+        functools.partial(gather_kernel, blks // 2),
+        out_shape=[
+            shape((blks * rows, heads // 2 * mixed), BF16),
+            shape((blks * rows, heads * wide), BF16),
+            shape((2, blks * rows, heads * gateup.shape[2]), BF16),
+            shape((blks * deep, heads * wide), BF16),
+        ],
+        in_specs=[vmem, vmem, vmem, ANYWHERE, vmem],
+        out_specs=[ANYWHERE] * 4,
+        scratch_shapes=[
+            pltpu.VMEM((rows // 2, wide), BF16),
+            pltpu.VMEM((2, rows // 2, narrow), BF16),
+            pltpu.VMEM((rows // 2, wide), BF16),
+            pltpu.VMEM((deep // 2, wide), BF16),
+            pltpu.VMEM((rows // 2, mixed), BF16),
+            pltpu.VMEM((rows // 2, 2 * wide), BF16),
+            pltpu.VMEM((deep // 2, 2 * wide), BF16),
+            dma((4,)),
+            dma((4,)),
+            dma((5,)),
+            *Spread.semaphores(5, blks // 2),
+        ],
+        compiler_params=pltpu.CompilerParams(
+            collective_id=0, has_side_effects=True, vmem_limit_bytes=24 << 20
+        ),
+    )(query, keyval, output, gateup, down)
+
+
+def windows(blocks, span, low_part):
+    reach = WINDOW + TILE
+    fixed = [(0, (block + 1) * span) for block in range(WINDOW // span)]
+    offset = TILE * (low_part // 2 + 1) - reach
+    return fixed, reach, offset
+
+
+def tiles_of(ref, flipped):
+    lane = lax.broadcasted_iota(jnp.int32, (ref.shape[0], TILE), 1)
+    result = []
+    for slot in range(4):
+        tile = ref[:, slot // 2 * TILE : (slot // 2 + 1) * TILE].astype(F32)
+        if (slot % 2 == 0) == flipped:
+            tile = pltpu.roll(tile, HEAD_DIM, 1)
+        keep = lane >= HEAD_DIM if flipped else lane < HEAD_DIM
+        result.append(jnp.where(keep, tile, 0.0).astype(BF16))
+    return result
+
+
+def joined(rows, flipped):
+    span = rows.shape[0] // 4
+    heads = [rows[slot * span : (slot + 1) * span] for slot in range(4)]
+    lane = lax.broadcasted_iota(jnp.int32, (span, TILE), 1)
+    result = []
+    for first, second in ((heads[0], heads[1]), (heads[2], heads[3])):
+        if flipped:
+            first = pltpu.roll(first, HEAD_DIM, 1)
+        else:
+            second = pltpu.roll(second, HEAD_DIM, 1)
+        result.append(jnp.where(lane < HEAD_DIM, first, second))
+    return result
+
+
+def bias_of(limits_ref, block, start, count):
+    key = start + lax.broadcasted_iota(jnp.int32, (count, TILE), 0)
+    least = limits_ref[0, pl.ds(block, 1), :]
+    most = limits_ref[1, pl.ds(block, 1), :]
+    self_pos = limits_ref[2, pl.ds(block, 1), :]
+    allowed = ((key >= least) & (key <= most)) | (key == self_pos)
+    bias = jnp.where(allowed, 0.0, MASKED)
+    return jnp.concatenate([bias, bias], axis=1)
+
+
+def each_block(blocks, body):
+    span = 4 * HEAD_DIM
+    fixed, reach, offset = windows(blocks, span, lax.axis_index("head"))
+    for block, (start, count) in enumerate(fixed):
+        body(block, start, count)
+
+    @pl.loop(len(fixed), blocks)
+    def _(block):
+        body(block, pl.multiple_of(block * span + offset, TILE), reach)
+
+
+def attend_kernel(limits_ref, q_ref, kv_ref, out_ref, lse_ref, q_rows, kv_turned):
+    blocks, span = q_rows.shape[0], q_rows.shape[2]
+    for slot, tile in enumerate(tiles_of(q_ref, False)):
+        q_rows[:, slot] = (tile * BF16(HEAD_DIM**-0.5)).reshape(blocks, span, TILE)
+    kv_turned[...] = kv_ref[...].astype(F32).T.astype(BF16)
+
+    def body(block, start, count):
+        queries = q_rows[block].reshape(4 * span, TILE)
+        scores = dot(kv_ref[pl.ds(start, count), :], queries, 1, 1)
+        scores = scores + bias_of(limits_ref, block, start, count)
+        top = jnp.max(scores, axis=0, keepdims=True)
+        shifted = jnp.exp(scores - top)
+        total = jnp.sum(shifted, axis=0, keepdims=True)
+        result = dot(kv_turned[:, pl.ds(start, count)], shifted.astype(BF16))
+        lse_ref[0, pl.ds(block, 1), :] = top + jnp.log(total)
+        result = (result / total).T
+        for at, tile in enumerate(joined(result, True)):
+            out_ref[pl.ds(block * span, span), at * TILE : (at + 1) * TILE] = tile.astype(BF16)
+
+    each_block(blocks, body)
+
+
+def attend(limits, queries, pairs):
+    rows, width = queries.shape
+    blocks = limits.shape[1]
+    groups = width // (2 * TILE)
+    return pl.pallas_call(
+        attend_kernel,
+        grid=(groups,),
+        out_shape=[
+            jax.ShapeDtypeStruct((rows, width), BF16),
+            jax.ShapeDtypeStruct((groups, blocks, 2 * TILE), F32),
+        ],
+        in_specs=[
+            pl.BlockSpec(limits.shape, lambda m: (0, 0, 0)),
+            pl.BlockSpec((rows, 2 * TILE), lambda m: (0, m)),
+            pl.BlockSpec((pairs.shape[0], TILE), lambda m: (0, m)),
+        ],
+        out_specs=[
+            pl.BlockSpec((rows, 2 * TILE), lambda m: (0, m)),
+            pl.BlockSpec((1, blocks, 2 * TILE), lambda m: (m, 0, 0)),
+        ],
+        scratch_shapes=[
+            pltpu.VMEM((blocks, 4, rows // blocks, TILE), BF16),
+            pltpu.VMEM((TILE, pairs.shape[0]), BF16),
+        ],
+        compiler_params=pltpu.CompilerParams(vmem_limit_bytes=48 << 20),
+    )(limits, queries, pairs)
+
+
+def attend_back_kernel(
+    limits_ref, q_ref, kv_ref, lse_ref, grad_ref, dq_ref, dkv_ref, q_rows, g_rows, kv_turned, total
+):
+    blocks, span = q_rows.shape[0], q_rows.shape[2]
+    scale = HEAD_DIM**-0.5
+    for slot, tile in enumerate(tiles_of(q_ref, False)):
+        q_rows[:, slot] = (tile * BF16(scale)).reshape(blocks, span, TILE)
+    for slot, tile in enumerate(tiles_of(grad_ref, True)):
+        g_rows[:, slot] = tile.reshape(blocks, span, TILE)
+    kv_turned[...] = kv_ref[...].astype(F32).T.astype(BF16)
+    total[...] = jnp.zeros_like(total)
+
+    def body(block, start, count):
+        keys = pl.ds(start, count)
+        queries = q_rows[block].reshape(4 * span, TILE)
+        grads = g_rows[block].reshape(4 * span, TILE)
+        scores = dot(kv_ref[keys, :], queries, 1, 1)
+        scores = scores + bias_of(limits_ref, block, start, count)
+        probs = jnp.exp(scores - lse_ref[0, pl.ds(block, 1), :])
+        grad_probs = dot(kv_ref[keys, :], grads, 1, 1)
+        inner = jnp.sum(probs * grad_probs, axis=0, keepdims=True)
+        grad_scores = (probs * (grad_probs - inner)).astype(BF16)
+        total[keys, :] += dot(grad_scores, queries) + dot(probs.astype(BF16), grads)
+        grad_q = (dot(kv_turned[:, keys], grad_scores) * scale).T
+        for at, tile in enumerate(joined(grad_q, False)):
+            dq_ref[pl.ds(block * span, span), at * TILE : (at + 1) * TILE] = tile
+
+    each_block(blocks, body)
+    dkv_ref[...] = total[...]
+
+
+def attend_back(limits, queries, pairs, lse, grads):
+    rows, width = queries.shape
+    blocks = limits.shape[1]
+    groups = width // (2 * TILE)
+    wide = pl.BlockSpec((rows, 2 * TILE), lambda m: (0, m))
+    long = pl.BlockSpec((pairs.shape[0], TILE), lambda m: (0, m))
+    each = pltpu.VMEM((blocks, 4, rows // blocks, TILE), BF16)
+    return pl.pallas_call(
+        attend_back_kernel,
+        grid=(groups,),
+        out_shape=[
+            jax.ShapeDtypeStruct((rows, width), F32),
+            jax.ShapeDtypeStruct(pairs.shape, F32),
+        ],
+        in_specs=[
+            pl.BlockSpec(limits.shape, lambda m: (0, 0, 0)),
+            wide,
+            long,
+            pl.BlockSpec((1, blocks, 2 * TILE), lambda m: (m, 0, 0)),
+            wide,
+        ],
+        out_specs=[wide, long],
+        scratch_shapes=[
+            each,
+            each,
+            pltpu.VMEM((TILE, pairs.shape[0]), BF16),
+            pltpu.VMEM((pairs.shape[0], TILE), F32),
+        ],
+        compiler_params=pltpu.CompilerParams(vmem_limit_bytes=48 << 20),
+    )(limits, queries, pairs, lse, grads)
+
+
+def by_sequence(
+    tokens,
+    attn_gain,
+    ffn_gain,
+    query_weight,
+    keyval_weight,
+    output_weight,
+    gateup_weight,
+    down_weight,
+    query_down,
+    query_up,
+    keyval_down,
+    keyval_up,
+    output_down,
+    output_up,
+    gateup_down,
+    gateup_up,
+    ffdown_down,
+    ffdown_up,
+    segment_ids,
+    real_mask,
+    adapter_index,
+    out_grad,
+):
+    seqs, part, width = tokens.shape
+    groups = lax.axis_size("head")
+    seq, head_pos = lax.axis_index("blk"), lax.axis_index("head")
+    rows = seqs * part
+    span = groups * part
+    adapter = adapter_index[seq]
+
+    def moved(array):
+        return lax.all_to_all(array, "blk", split_axis=0, concat_axis=0, tiled=True)
+
+    flat = moved(tokens).reshape(rows, width).astype(F32)
+    grad_flat = moved(out_grad).reshape(rows, width)
+    w_qkv, w_output, w_gateup, w_down = gather_weights(
+        query_weight, keyval_weight, output_weight, gateup_weight, down_weight
+    )
+    d_query = query_down.swapaxes(1, 2)[adapter]
+    d_keyval = keyval_down.swapaxes(2, 3)[adapter]
+    d_output = output_down.swapaxes(1, 2)[adapter]
+    d_gateup = gateup_down.swapaxes(2, 3)[adapter]
+    d_ffdown = ffdown_down.swapaxes(1, 2)[adapter]
+    u_query, u_keyval, u_output = query_up[adapter], keyval_up[adapter], output_up[adapter]
+    u_gateup, u_ffdown = gateup_up[adapter], ffdown_up[adapter]
+    rank = d_query.shape[0]
+
+    half, narrow = width // 2, u_keyval.shape[2] // 2
+    mixed = w_qkv.shape[1] // 2
+    fill = mixed - half - 2 * narrow
+
+    def interleaved(query, key, value):
+        empty = jnp.zeros(query.shape[:-1] + (fill,), query.dtype)
+        pieces = []
+        for y in (0, 1):
+            pieces += [
+                query[:, y * half : (y + 1) * half],
+                key[:, y * narrow : (y + 1) * narrow],
+                value[:, y * narrow : (y + 1) * narrow],
+                empty,
+            ]
+        return jnp.concatenate(pieces, axis=1)
+
+    def separated(array):
+        def at(begin, size):
+            return jnp.concatenate(
+                [array[:, y * mixed + begin : y * mixed + begin + size] for y in (0, 1)], axis=1
+            )
+
+        return at(0, half), at(half, narrow), at(half + narrow, narrow)
+
+    nil_q, nil_k = jnp.zeros_like(u_query), jnp.zeros_like(u_keyval[0])
+    u_qkv = jnp.concatenate(
+        [
+            interleaved(u_query, nil_k, nil_k),
+            interleaved(nil_q, u_keyval[0], nil_k),
+            interleaved(nil_q, nil_k, u_keyval[1]),
+        ],
+        axis=0,
+    )
+    d_qkv = jnp.concatenate([d_query, d_keyval[0], d_keyval[1]], axis=0)
+
+    def project(inputs, weight, down, up):
+        lowered = dot(inputs, down, 1, 1).astype(BF16)
+        return dot(inputs, weight) + ADAPTER_SCALE * dot(lowered, up), lowered
+
+    def project_back(inputs, lowered, grad, weight, down, up):
+        grad_up = ADAPTER_SCALE * dot(lowered, grad, 0, 0)
+        grad_low = (ADAPTER_SCALE * dot(grad, up, 1, 1)).astype(BF16)
+        grad_down = dot(grad_low, inputs, 0, 0)
+        return dot(grad, weight, 1, 1) + dot(grad_low, down), grad_down, grad_up
+
+    def norm(values, gain):
+        inverse = lax.rsqrt(jnp.mean(values * values, axis=-1, keepdims=True) + EPSILON)
+        return (values * inverse * gain).astype(BF16), inverse
+
+    def norm_back(values, inverse, gain, grad):
+        weighted = grad * gain
+        mean = jnp.mean(values * weighted, axis=-1, keepdims=True)
+        return inverse * weighted - values * (inverse * inverse * inverse * mean)
+
+    position = (
+        jnp.arange(seqs, dtype=jnp.int32)[:, None] * span
+        + head_pos * part
+        + jnp.arange(part, dtype=jnp.int32)[None, :]
+    )
+    length = jnp.sum(real_mask[seq])
+    segment = segment_ids[seq]
+    mine = jnp.take(segment, position)
+    first = jnp.sum((segment[None, None, :] < mine[:, :, None]).astype(jnp.int32), axis=2)
+    least = jnp.maximum(position - (WINDOW - 1), first)
+    most = jnp.minimum(position, length - 1)
+    limits = jnp.stack([least, most, position])
+    limits = jnp.concatenate([limits, limits], axis=2)
+
+    normed, inverse1 = norm(flat, attn_gain)
+    qkv, low_qkv = project(normed, w_qkv, d_qkv, u_qkv)
+    queries, keys, values = separated(qkv)
+    flat_pos = position.reshape(rows)
+    heads, kv_heads = HEADS, KV_HEADS
+    queries = rotate(queries.reshape(rows, heads, HEAD_DIM), flat_pos, 1.0)
+    queries = queries.astype(BF16).reshape(rows, width)
+    keys = rotate(keys.reshape(rows, kv_heads, HEAD_DIM), flat_pos, 1.0).astype(BF16)
+    values = values.reshape(rows, kv_heads, HEAD_DIM).astype(BF16)
+    pairs = jnp.concatenate([keys, values], axis=2).reshape(seqs, part, 2 * kv_heads * HEAD_DIM)
+    pairs = lax.all_gather(pairs, "head", axis=1, tiled=True)
+    pairs = pairs.reshape(seqs * span, 2 * kv_heads * HEAD_DIM)
+    attended, lse = attend(limits, queries, pairs)
+
+    branch, low_output = project(attended, w_output, d_output, u_output)
+    middle = flat + branch
+    normed2, inverse2 = norm(middle, ffn_gain)
+    gate, low_gate = project(normed2, w_gateup[0], d_gateup[0], u_gateup[0])
+    upward, low_upward = project(normed2, w_gateup[1], d_gateup[1], u_gateup[1])
+    sigma = jax.nn.sigmoid(gate)
+    silu = gate * sigma
+    activated = (silu * upward).astype(BF16)
+    branch, low_ffdown = project(activated, w_down, d_ffdown, u_ffdown)
+    output = (middle + branch).astype(BF16)
+
+    grad_act, gd_ffdown, gu_ffdown = project_back(
+        activated, low_ffdown, grad_flat, w_down, d_ffdown, u_ffdown
+    )
+    grad_gate = (grad_act * upward * (sigma * (1.0 + gate * (1.0 - sigma)))).astype(BF16)
+    grad_upward = (grad_act * silu).astype(BF16)
+    grad_in_gate, gd_gate, gu_gate = project_back(
+        normed2, low_gate, grad_gate, w_gateup[0], d_gateup[0], u_gateup[0]
+    )
+    grad_in_up, gd_up, gu_up = project_back(
+        normed2, low_upward, grad_upward, w_gateup[1], d_gateup[1], u_gateup[1]
+    )
+    grad_middle = grad_flat.astype(F32) + norm_back(
+        middle, inverse2, ffn_gain, grad_in_gate + grad_in_up
+    )
+    grad_mixed, gd_output, gu_output = project_back(
+        attended, low_output, grad_middle.astype(BF16), w_output, d_output, u_output
+    )
+    grad_query, grad_pairs = attend_back(limits, queries, pairs, lse, grad_mixed.astype(BF16))
+    grad_pairs = lax.psum_scatter(
+        grad_pairs.reshape(seqs, span, -1), "head", scatter_dimension=1, tiled=True
+    ).reshape(rows, kv_heads, 2 * HEAD_DIM)
+    grad_query = rotate(grad_query.reshape(rows, heads, HEAD_DIM), flat_pos, -1.0)
+    grad_keys = rotate(grad_pairs[:, :, :HEAD_DIM], flat_pos, -1.0)
+    grad_values = grad_pairs[:, :, HEAD_DIM:]
+    grad_qkv = interleaved(
+        grad_query.astype(BF16).reshape(rows, width),
+        grad_keys.astype(BF16).reshape(rows, kv_heads * HEAD_DIM),
+        grad_values.astype(BF16).reshape(rows, kv_heads * HEAD_DIM),
+    )
+    grad_normed, gd_qkv, gu_qkv = project_back(normed, low_qkv, grad_qkv, w_qkv, d_qkv, u_qkv)
+    input_grad = grad_middle + norm_back(flat, inverse1, attn_gain, grad_normed)
+
+    gu_query = separated(gu_qkv[:rank])[0]
+    gu_key = separated(gu_qkv[rank : 2 * rank])[1]
+    gu_value = separated(gu_qkv[2 * rank :])[2]
+    terms = [
+        gd_qkv[:rank],
+        gu_query,
+        gd_qkv[rank : 2 * rank],
+        gd_qkv[2 * rank :],
+        gu_key,
+        gu_value,
+        gd_output,
+        gu_output,
+        gd_gate,
+        gd_up,
+        gu_gate,
+        gu_up,
+        gd_ffdown,
+        gu_ffdown,
+    ]
+    sizes = [term.shape[1] for term in terms]
+    unit = groups * TILE
+    extra = -sum(sizes) % unit
+    terms.append(jnp.zeros((rank, extra), F32))
+    shared = lax.psum_scatter(
+        jnp.concatenate(terms, axis=1), "head", scatter_dimension=1, tiled=True
+    )
+    shared = lax.all_gather(shared.astype(BF16), ("blk", "head"), axis=0)
+    shared = shared.reshape(seqs, groups, rank, -1).swapaxes(1, 2).reshape(seqs, rank, -1)
+    adapters = jnp.arange(query_down.shape[0], dtype=jnp.int32)
+    holder = jnp.argmax(adapter_index[None, :] == adapters[:, None], axis=1)
+    shared = shared[holder]
+    cuts = np.cumsum([0] + sizes)
+    found = [shared[:, :, begin:end].astype(F32) for begin, end in zip(cuts[:-1], cuts[1:])]
+    return (
+        moved(output.reshape(seqs, part, width)),
+        moved(input_grad.astype(BF16).reshape(seqs, part, width)),
+        found[0].swapaxes(1, 2),
+        found[1],
+        jnp.stack([found[2], found[3]], axis=1).swapaxes(2, 3),
+        jnp.stack([found[4], found[5]], axis=1),
+        found[6].swapaxes(1, 2),
+        found[7],
+        jnp.stack([found[8], found[9]], axis=1).swapaxes(2, 3),
+        jnp.stack([found[10], found[11]], axis=1),
+        found[12].swapaxes(1, 2),
+        found[13],
+    )
+
+
 def solution(mesh):
     in_specs = (
         P(None, ("blk", "head"), None),
@@ -436,6 +1167,12 @@
         P(),
         P(),
     )
+
+    def chosen(tokens, *rest):
+        if mesh.shape["blk"] == tokens.shape[0] == 8 and mesh.shape["head"] == 4:
+            return by_sequence(tokens, *rest)
+        return on_device(tokens, *rest)
+
     return jax.shard_map(
-        on_device, mesh=mesh, in_specs=in_specs, out_specs=out_specs, check_vma=False
-    )
+        chosen, mesh=mesh, in_specs=in_specs, out_specs=out_specs, check_vma=False
+    )

time: 1750 us -> 700 us (0.40)
  waiting for transfers between devices: 553 us -> 88.3 us
  local copies, waits for them, and re-layouts: 469 us -> 100 us
  matrix products: 385 us -> 137 us
  Pallas kernels: 0 us -> 246 us
  blocking collectives: 140 us -> 50.4 us
  other arithmetic: 117 us -> 31.2 us
  starting transfers between devices: 49.6 us -> 18.3 us
    ppermute x8 -> x0, waiting for transfers between devices: 314 us -> none  [passed_along(): lax.ppermute(value, axis, [(source, source + steps) for source in range(i...]
    dot_general x116 -> x40, matrix products: 385 us -> 137 us  [dot(): lax.dot_general(left, right, (((left_dim,), (right_dim,)), ((), ())), pre...]
    pallas_call x0 -> x3, Pallas kernels: none -> 246 us  [the longest x1 173 us: gather_weights(): pl.pallas_call(functools.partial(gather_kernel, blks // 2), out_shape=[sh...]
    psum x1 -> x0, waiting for transfers between devices: 215 us -> none  [on_device(): lax.psum((per_adapter(gd_query), per_adapter(gu_query), per_adapter(jnp.s...]
    unnamed x238 -> x154, local copies, waits for them, and re-layouts: 190 us -> 37.1 us
    all_gather x3 -> x0, blocking collectives: 104 us -> none  [the longest x1 37.3 us: on_device(): lax.all_gather(output_weight, 'blk', axis=0, tiled=True)]
    another operation x8 -> x5, local copies, waits for them, and re-layouts: 72 us -> 0.11 us  [the longest x1 0.1 us: by_sequence(): jnp.stack([found[4], found[5]], axis=1)]
    reduce_scatter x0 -> x2, waiting for transfers between devices: none -> 59.2 us  [the longest x1 31.6 us: by_sequence(): lax.psum_scatter(grad_pairs.reshape(seqs, span, -1), 'head', scatter_dime...]
  transfers between devices with their start and end apart: 21 -> 7, of which waited for: 10 -> 3; matrix products, arithmetic and copies ran while one was open for 34% -> 14% of each run, Pallas kernels for 0% -> 25%
where the time goes in v1:
time: 700 us; the launch traced here: 689 us
  Pallas kernels  246 us (35%)
  matrix products  137 us (20%)
  local copies, waits for them, and re-layouts  100 us (14%)
  waiting for transfers between devices  88.3 us (13%)
  blocking collectives  50.4 us (7%)
  other arithmetic  31.2 us (4%)
  starting transfers between devices  18.3 us (3%)
  between operations  17.5 us (2%)
    pallas_call x1, Pallas kernels, gather_weights(): pl.pallas_call(functools.partial(gather_kernel, blks // 2), out_shape=[sh...  173 us
    dot_general x40, matrix products, dot(): lax.dot_general(left, right, (((left_dim,), (right_dim,)), ((), ())), pre...  137 us
    all_to_all x1, blocking collectives, moved(): return lax.all_to_all(array, 'blk', split_axis=0, concat_axis=0, tiled=True)  50.4 us
    pallas_call x1, Pallas kernels, attend_back(): pl.pallas_call(attend_back_kernel, grid=(groups,), out_shape=[jax.ShapeDt...  41.3 us
    unnamed x154, local copies, waits for them, and re-layouts  37.1 us
    reduce_scatter x1, waiting for transfers between devices, by_sequence(): lax.psum_scatter(grad_pairs.reshape(seqs, span, -1), 'head', scatter_dime...  31.6 us
    pallas_call x1, Pallas kernels, attend(): pl.pallas_call(attend_kernel, grid=(groups,), out_shape=[jax.ShapeDtypeSt...  31.3 us
    all_to_all x3, waiting for transfers between devices, moved(): return lax.all_to_all(array, 'blk', split_axis=0, concat_axis=0, tiled=True)  29.1 us
  transfers between devices with their start and end apart: 7, of which 3 were waited for; matrix products, arithmetic and copies ran while one was open for 14% of the time, Pallas kernels for 25%

profile of v1, /device:TPU:0, one launch (start us, length us, event | category | flops | bytes accessed | tf_op | source)
XLA Modules:
  0.0 689.0 jit_solution(6465135355871174186)
XLA Ops:
  7.2 7.4 %all-to-all-start = ((bf16[8,64,1280]{2,1,0:T(8,128)(2,1)}), bf16[8,64,1280]{2,1,0:T(8,128)(2,1)}, u32[]{:S(2)}, u32[]{:S(2)}) async-start(bf16[8,64,1280]{2,1,0:T(8,128)(2,1)} %param.22), calls=%async_computation | async-start | bytes 2621440 | tf_op jit(solution)/shard_map/all_to_all | solution.py:941
  25.8 173.3 %shard_map.301 = (bf16[1280,2048]{1,0:T(8,128)(2,1)S(1)}, bf16[1280,1280]{1,0:T(8,128)(2,1)S(1)}, bf16[2,1280,3584]{2,1,0:T(8,128)(2,1)}, bf16[3584,1280]{1,0:T(8,128)(2,1)S(1)}) custom-call(bf16[160,320]{1,0:T(8,128)(2,1)S(1)} %copy-done.8, bf16[2,160,80]{2,1,0:T(8,128)(2,1)S(1)} %copy-done.10, bf16[160,320]{1,0:T(8,128)(2,1)S(1)} %copy-done.9, ...), custom_call_target="tpu_custom_call" | custom-call | tf_op jit(solution)/shard_map/pallas_call | solution.py:713
  210.0 5.0 all-to-all-start.2
  218.5 5.4 fusion.107
  251.7 11.9 %fusion.110 = f32[3584,512]{0,1:T(8,128)} fusion(bf16[3584,1280]{1,0:T(8,128)(2,1)} %copy-done.11, bf16[512,1280]{1,0:T(8,128)(2,1)} %bitcast.31), kind=kOutput, calls=%fused_computation.215 | convolution fusion | flops 4697620480 | bytes 17825792 | tf_op jit(solution)/shard_map/dot_general | solution.py:411
  265.4 31.3 %shard_map.302 = (bf16[512,1280]{1,0:T(8,128)(2,1)S(1)}, f32[5,8,256]{2,1,0:T(8,128)S(1)}) custom-call(s32[3,8,128]{2,1,0:T(8,128)S(1)} %add_add_fusion.limits_ref, bf16[512,1280]{1,0:T(8,128)(2,1)S(1)} %copy.62.q_ref, bf16[2048,640]{1,0:T(8,128)(2,1)S(1)} %bitcast.209), custom_call_target="tpu_custom_call" | custom-call | tf_op jit(solution)/shard_map/pallas_call | solution.py:822
  309.1 11.9 %multiply_add_fusion = f32[512,3584]{1,0:T(8,128)} fusion(f32[512,3584]{1,0:T(8,128)} %fusion.53, bf16[512,1280]{1,0:T(8,128)(2,1)S(1)} %multiply_convert_fusion.3, bf16[2,1280,3584]{2,1,0:T(8,128)(2,1)} %get-tuple-element.24), kind=kOutput, calls=%fused_computation.18 | convolution fusion | flops 4701290496 | bytes 25165824 | tf_op jit(solution)/shard_map/dot_general | solution.py:411
  320.9 10.6 %multiply_add_fusion.1 = f32[512,3584]{1,0:T(8,128)} fusion(f32[512,3584]{1,0:T(8,128)S(1)} %fusion.50, bf16[512,1280]{1,0:T(8,128)(2,1)S(1)} %multiply_convert_fusion.3, bf16[2,1280,3584]{2,1,0:T(8,128)(2,1)} %get-tuple-element.24), kind=kOutput, calls=%fused_computation.21 | convolution fusion | flops 4701290496 | bytes 25165824 | tf_op jit(solution)/shard_map/dot_general | solution.py:411
  331.5 11.4 %multiply_convert_fusion = (bf16[512,3584]{1,0:T(8,128)(2,1)}, bf16[512,3584]{1,0:T(8,128)(2,1)S(1)}, bf16[512,3584]{1,0:T(8,128)(2,1)}) fusion(f32[512,3584]{1,0:T(8,128)} %multiply_add_fusion.1, f32[512,3584]{1,0:T(8,128)} %multiply_add_fusion, bf16[16,512]{1,0:T(8,128)(2,1)S(1)} %fusion.44, bf16[8,3584,16]{1,2,0:T(8,128)(2,1)} %param.38, ...), kind=kOutput, calls=%fused_computation.15 | convolution fusion | flops 88080384 | bytes 33161220 | tf_op jit(solution)/shard_map/dot_general | solution.py:411
  342.9 4.4 fusion.47
  349.0 9.5 %fusion.17 = f32[512,1280]{1,0:T(8,128)} fusion(f32[512,1280]{1,0:T(8,128)S(1)} %fusion.60, bf16[512,3584]{1,0:T(8,128)(2,1)S(1)} %get-tuple-element.67, bf16[2,1280,3584]{2,1,0:T(8,128)(2,1)} %get-tuple-element.24), kind=kOutput, calls=%fused_computation.27 | convolution fusion | flops 4698275840 | bytes 18087936 | tf_op jit(solution)/shard_map/dot_general | solution.py:411
  360.4 11.0 %multiply_reduce_fusion = (f32[512]{0:T(512)S(1)}, f32[512,1280]{1,0:T(8,128)}) fusion(f32[512,1280]{1,0:T(8,128)S(1)} %get-tuple-element.129, f32[1280]{0:T(1024)S(1)} %copy-done.65, f32[512,1280]{1,0:T(8,128)} %fusion.17, f32[512,1280]{1,0:T(8,128)} %fusion.61, bf16[512,3584]{1,0:T(8,128)(2,1)S(1)} %copy-done.26, bf16[2,1280,3584]{2,1,0:T(8,128)(2,1)} %get-tuple-element.24), kind=kOutput, calls=%fused_computation.55 | convolution fusion | flops 4700896768 | bytes 23337984 | tf_op jit(solution)/shard_map/dot_general | solution.py:411
  378.7 41.3 %shard_map.303 = (f32[512,1280]{1,0:T(8,128)S(1)}, f32[2048,640]{1,0:T(8,128)}) custom-call(s32[3,8,128]{2,1,0:T(8,128)S(1)} %add_add_fusion.limits_ref, bf16[512,1280]{1,0:T(8,128)(2,1)S(1)} %copy.62.q_ref, bf16[2048,640]{1,0:T(8,128)(2,1)} %bitcast.208, f32[5,8,256]{2,1,0:T(8,128)S(1)} %get-tuple-element.26.lse_ref, bf16[512,1280]{1,0:T(8,128)(2,1)S(1)} %fusion.34.grad_ref), custom_call_target="tpu_custom_call" | custom-call | tf_op jit(solution)/shard_map/pallas_call | solution.py:884
  443.0 31.6 %reduce-scatter.3.cloned.1.call-done = f32[8,64,640]{2,1,0:T(8,128)} async-done(((f32[8,256,640]{2,1,0:T(8,128)}), f32[8,64,640]{2,1,0:T(8,128)}) %reduce-scatter.3.cloned.1.call-update) | async-done | bytes 1310736 | tf_op jit(solution)/shard_map/reduce_scatter | solution.py:1068
  477.2 5.0 fusion.98
  506.5 27.6 %reduce-scatter.5.cloned.1.call-done = f32[16,5760]{1,0:T(8,128)} async-done(((f32[16,23040]{1,0:T(8,128)}), f32[16,5760]{1,0:T(8,128)}) %reduce-scatter.5.cloned.1.call-update) | async-done | bytes 368656 | tf_op jit(solution)/shard_map/reduce_scatter | solution.py:1105
  535.8 9.7 %fusion.109 = f32[512,1280]{1,0:T(8,128)S(1)} fusion(bf16[512,3584]{1,0:T(8,128)(2,1)} %get-tuple-element.68, bf16[3584,1280]{1,0:T(8,128)(2,1)} %copy-done.11), kind=kOutput, calls=%fused_computation.214 | convolution fusion | flops 4697620480 | bytes 15466496 | tf_op jit(solution)/shard_map/dot_general | solution.py:411
  548.0 5.7 all-to-all-start.1
  553.8 6.1 fusion.111
  564.9 29.0 %all-to-all-done.1 = bf16[8,64,1280]{2,1,0:T(8,128)(2,1)} async-done(((bf16[8,64,1280]{2,1,0:T(8,128)(2,1)}), bf16[8,64,1280]{2,1,0:T(8,128)(2,1)}, u32[]{:S(2)}, u32[]{:S(2)}) %all-to-all-start.1) | async-done | bytes 1310752 | tf_op jit(solution)/shard_map/all_to_all | solution.py:941
  594.0 50.4 %all_to_all.20 = bf16[8,64,1280]{2,1,0:T(8,128)(2,1)S(1)} all-to-all(bf16[8,64,1280]{2,1,0:T(8,128)(2,1)} %bitcast.216), channel_id=1, replica_groups=mesh['blk'=8,'head'=4] {'blk'}, dimensions={0} | all-to-all | bytes 2621440 | tf_op jit(solution)/shard_map/all_to_all | solution.py:941
  644.3 7.6 %copy.78 = bf16[8,4,16,5760]{3,1,2,0:T(4,128)(2,1)} copy(bf16[8,4,16,5760]{3,2,1,0:T(8,128)(2,1)} %bitcast.215) | data formatting | bytes 11796480 | tf_op jit(solution)/shard_map/reshape | solution.py:1109
  652.0 8.7 %reshape.423 = bf16[8,16,23040]{2,1,0:T(8,128)(2,1)} reshape(bf16[8,16,4,5760]{3,2,1,0:T(4,128)(2,1)} %bitcast.212) | data formatting | bytes 11796480 | tf_op jit(solution)/shard_map/reshape | solution.py:1109
  660.7 6.2 gather_fusion.1
  (275 shorter events, 149.3 us)
Async XLA Ops:
  7.2 296.7 %copy-start = (bf16[8,2,16,3584]{3,2,1,0:T(8,128)(2,1)S(1)}, bf16[8,2,16,3584]{3,2,1,0:T(8,128)(2,1)}, u32[]{:S(2)}) copy-start(bf16[8,2,16,3584]{3,2,1,0:T(8,128)(2,1)} %param.37) | copy-start | bytes 5505028
  7.2 12.2 %copy-start.58 = (bf16[448,320]{0,1:T(8,128)(2,1)S(1)}, bf16[448,320]{0,1:T(8,128)(2,1)}, u32[]{:S(2)}) copy-start(bf16[448,320]{0,1:T(8,128)(2,1)} %param.29) | copy-start | bytes 860164
  7.2 202.8 %all-to-all-start = ((bf16[8,64,1280]{2,1,0:T(8,128)(2,1)}), bf16[8,64,1280]{2,1,0:T(8,128)(2,1)}, u32[]{:S(2)}, u32[]{:S(2)}) async-start(bf16[8,64,1280]{2,1,0:T(8,128)(2,1)} %param.22), calls=%async_computation | async-start | bytes 2621440 | tf_op jit(solution)/shard_map/all_to_all | solution.py:941
  14.6 10.0 %copy-start.66 = (s32[8]{0:T(128)}, s32[8]{0:T(128)S(1)}, u32[]{:S(2)}) copy-start(s32[8]{0:T(128)S(1)} %multiply_add_fusion.3) | copy-start | bytes 100
  24.7 199.8 %copy-start.42 = (bf16[16,2048]{1,0:T(8,128)(2,1)}, bf16[16,2048]{1,0:T(8,128)(2,1)S(1)}, u32[]{:S(2)}) copy-start(bf16[16,2048]{1,0:T(8,128)(2,1)S(1)} %concatenate.55) | copy-start | bytes 196612
  24.8 199.7 %copy-start.44 = (bf16[16,2048]{1,0:T(8,128)(2,1)}, bf16[16,2048]{1,0:T(8,128)(2,1)S(1)}, u32[]{:S(2)}) copy-start(bf16[16,2048]{1,0:T(8,128)(2,1)S(1)} %concatenate.56) | copy-start | bytes 196612
  25.8 198.7 %copy-start.46 = (bf16[16,2048]{1,0:T(8,128)(2,1)}, bf16[16,2048]{1,0:T(8,128)(2,1)S(1)}, u32[]{:S(2)}) copy-start(bf16[16,2048]{1,0:T(8,128)(2,1)S(1)} %concatenate.54) | copy-start | bytes 196612
  204.3 12.5 %copy-start.61 = (f32[1280]{0:T(1024)S(1)}, f32[1280]{0:T(1024)}, u32[]{:S(2)}) copy-start(f32[1280]{0:T(1024)} %param.23) | copy-start | bytes 15364
  207.4 16.5 %copy-start.50 = (bf16[16,1280]{1,0:T(8,128)(2,1)}, bf16[16,1280]{1,0:T(8,128)(2,1)S(1)}, u32[]{:S(2)}) copy-start(bf16[16,1280]{1,0:T(8,128)(2,1)S(1)} %dynamic-slice_bitcast_fusion.9) | copy-start | bytes 122884
  208.4 23.2 %copy-start.40 = (f32[512,32]{0,1:T(8,128)}, f32[512,32]{0,1:T(8,128)S(1)}, u32[]{:S(2)}) copy-start(f32[512,32]{0,1:T(8,128)S(1)} %get-tuple-element.119) | copy-start | bytes 196612
  210.0 13.9 %copy-start.52 = (bf16[16,1280]{1,0:T(8,128)(2,1)}, bf16[16,1280]{1,0:T(8,128)(2,1)S(1)}, u32[]{:S(2)}) copy-start(bf16[16,1280]{1,0:T(8,128)(2,1)S(1)} %get-tuple-element.110) | copy-start | bytes 122884
  210.0 13.9 %copy-start.54 = (bf16[16,1280]{1,0:T(8,128)(2,1)}, bf16[16,1280]{1,0:T(8,128)(2,1)S(1)}, u32[]{:S(2)}) copy-start(bf16[16,1280]{1,0:T(8,128)(2,1)S(1)} %get-tuple-element.111) | copy-start | bytes 122884
  210.0 39.9 %all-to-all-start.2 = ((bf16[8,64,1280]{2,1,0:T(8,128)(2,1)}), bf16[8,64,1280]{2,1,0:T(8,128)(2,1)}, u32[]{:S(2)}, u32[]{:S(2)}) async-start(bf16[8,64,1280]{2,1,0:T(8,128)(2,1)} %param.43), calls=%async_computation.2 | async-start | bytes 2621440 | tf_op jit(solution)/shard_map/all_to_all | solution.py:941
  215.0 48.6 %all-gather.4.cloned.1.call-start = ((), (), s32[]{:S(2)}) async-start(), calls=%async_computation.6 | async-start | bytes 3276800 | tf_op jit(solution)/shard_map/all_gather | solution.py:1035
  235.9 238.7 %reduce-scatter.3.cloned.1.call-start = ((), (), s32[]{:S(2)}) async-start(), calls=%async_computation.7 | async-start | bytes 6553600 | tf_op jit(solution)/shard_map/reduce_scatter | solution.py:1068
  265.4 31.3 %copy-start.14 = (bf16[1280,1280]{1,0:T(8,128)(2,1)S(1)}, bf16[1280,1280]{1,0:T(8,128)(2,1)}, u32[]{:S(2)}) copy-start(bf16[1280,1280]{1,0:T(8,128)(2,1)} %copy-done.13) | copy-start | bytes 9830404
  302.0 69.5 %copy-start.15 = (f32[512,1280]{1,0:T(8,128)}, f32[512,1280]{1,0:T(8,128)S(1)}, u32[]{:S(2)}) copy-start(f32[512,1280]{1,0:T(8,128)S(1)} %get-tuple-element.129) | copy-start | bytes 7864324
  302.3 18.6 %copy-start.19 = (bf16[512,1280]{1,0:T(8,128)(2,1)}, bf16[512,1280]{1,0:T(8,128)(2,1)S(1)}, u32[]{:S(2)}) copy-start(bf16[512,1280]{1,0:T(8,128)(2,1)S(1)} %multiply_convert_fusion.3) | copy-start | bytes 3932164
  349.0 11.5 %copy-start.26 = (bf16[512,3584]{1,0:T(8,128)(2,1)S(1)}, bf16[512,3584]{1,0:T(8,128)(2,1)}, u32[]{:S(2)}) copy-start(bf16[512,3584]{1,0:T(8,128)(2,1)} %get-tuple-element.66) | copy-start | bytes 11010052
  421.5 112.6 %reduce-scatter.5.cloned.1.call-start = ((), (), s32[]{:S(2)}) async-start(), calls=%async_computation.8 | async-start | bytes 1843200 | tf_op jit(solution)/shard_map/reduce_scatter | solution.py:1105
  506.4 137.9 %all-gather.6.cloned.1.call-start = ((), (), s32[]{:S(2)}) async-start(), calls=%async_computation.9 | async-start | bytes 6082560 | tf_op jit(solution)/shard_map/all_gather | solution.py:1108
  535.8 9.8 %copy-start.16 = (f32[512,1280]{1,0:T(8,128)S(1)}, f32[512,1280]{1,0:T(8,128)}, u32[]{:S(2)}) copy-start(f32[512,1280]{1,0:T(8,128)} %copy-done.15) | copy-start | bytes 7864324
  535.8 9.8 %copy-start.60 = (bf16[512,16]{0,1:T(8,128)(2,1)S(1)}, bf16[512,16]{0,1:T(8,128)(2,1)}, u32[]{:S(2)}) copy-start(bf16[512,16]{0,1:T(8,128)(2,1)} %copy-done.59) | copy-start | bytes 49156
  548.0 46.0 %all-to-all-start.1 = ((bf16[8,64,1280]{2,1,0:T(8,128)(2,1)}), bf16[8,64,1280]{2,1,0:T(8,128)(2,1)}, u32[]{:S(2)}, u32[]{:S(2)}) async-start(bf16[8,64,1280]{2,1,0:T(8,128)(2,1)} %bitcast.221), calls=%async_computation.1 | async-start | bytes 2621440 | tf_op jit(solution)/shard_map/all_to_all | solution.py:941
  (52 other events, 230.0 us)
Sparse Core Ops, SparseCore 0:
  236.0 26.9 all-gather.3
  421.6 52.9 reduce-scatter.2
  506.5 27.5 reduce-scatter.4
  537.5 100.3 all-gather.5

commit v2 on v1

--- a/solution.py
+++ b/solution.py
@@ -519,6 +519,9 @@
         )
 
     def piece(self, ref, which):
+        if ref.shape[0] < 32:
+            size = ref.shape[1] // 2
+            return ref.at[:, pl.ds(which * size, size)]
         begin, size = halves(ref.shape[0])[which]
         return ref.at[pl.ds(begin, size)]
 
@@ -628,33 +631,50 @@
     return [jnp.where(core == 0, own, other), jnp.where(core == 0, other, own)]
 
 
+def in_pairs(array):
+    half = array.shape[1] // 2
+    size = 2 * KV_HEADS * HEAD_DIM // 4
+    keys = jnp.concatenate([array[:, :size], array[:, half : half + size]], axis=1)
+    values = jnp.concatenate(
+        [array[:, size : 2 * size], array[:, half + size : half + 2 * size]], axis=1
+    )
+    pieces = []
+    for head in range(KV_HEADS):
+        cut = slice(head * HEAD_DIM, (head + 1) * HEAD_DIM)
+        pieces += [keys[:, cut], values[:, cut]]
+    return jnp.concatenate(pieces, axis=1)
+
+
 def gather_kernel(lines, *refs):
     query, keyval, output, gateup, down, w_qkv, w_output, w_gateup, w_down = refs[:9]
-    got_query, got_keyval, got_output, got_down, my_qkv, my_output, my_down = refs[9:16]
-    pair_out, pair_in, local = refs[16:19]
-    rows, deep = my_qkv.shape[0], my_down.shape[0]
-    wide, mixed = my_output.shape[1], my_qkv.shape[1]
+    got_query, got_keyval, got_output, got_down, my_query, my_keyval, my_output, my_down = refs[9:17]
+    all_keyval, pairs, pair_out, pair_in, local = refs[17:22]
+    rows, deep = my_query.shape[0], my_down.shape[0]
+    wide, mixed = my_output.shape[1], my_keyval.shape[1]
     span, hidden = gateup.shape[1:]
+    width = w_output.shape[1]
 
     def target(part, z, x, y, core):
         blk, head = z * 2 + x, y * 2 + core
         if part == 0:
-            return w_qkv.at[pl.ds(blk * 2 * rows + core * rows, rows), pl.ds(y * mixed, mixed)]
+            return all_keyval.at[pl.ds(blk * 2 * rows + core * rows, rows), pl.ds(y * mixed, mixed)]
         if part == 1:
+            return w_qkv.at[pl.ds(blk * 2 * rows + core * rows, rows), pl.ds(y * wide, wide)]
+        if part == 2:
             return w_output.at[pl.ds(blk * 2 * rows + core * rows, rows), pl.ds(y * wide, wide)]
-        if part == 4:
+        if part == 5:
             return w_down.at[pl.ds(blk * 2 * deep + core * deep, deep), pl.ds(y * wide, wide)]
-        return w_gateup.at[part - 2, pl.ds(blk * span, span), pl.ds(head * hidden, hidden)]
-
-    sources = [my_qkv, my_output, gateup.at[0], gateup.at[1], my_down]
-    spread = Spread(sources, target, lines, refs[19:])
+        return w_gateup.at[part - 3, pl.ds(blk * span, span), pl.ds(head * hidden, hidden)]
+
+    sources = [my_keyval, my_query, my_output, gateup.at[0], gateup.at[1], my_down]
+    spread = Spread(sources, target, lines, refs[22:])
     core = spread.core
     spread.greet()
     sibling = device(spread.z, spread.x, spread.y, 1 - core)
     theirs = pl.ds((1 - core) * rows, rows)
     swaps = [
-        spread.copy(query.at[theirs], got_query, pair_out.at[0], pair_in.at[0], sibling),
-        spread.copy(keyval.at[:, theirs], got_keyval, pair_out.at[1], pair_in.at[1], sibling),
+        spread.copy(keyval.at[:, theirs], got_keyval, pair_out.at[0], pair_in.at[0], sibling),
+        spread.copy(query.at[theirs], got_query, pair_out.at[1], pair_in.at[1], sibling),
         spread.copy(output.at[theirs], got_output, pair_out.at[2], pair_in.at[2], sibling),
         spread.copy(
             down.at[pl.ds((1 - core) * deep, deep)], got_down, pair_out.at[3], pair_in.at[3], sibling
@@ -664,41 +684,50 @@
         swap.start()
     mine = pl.ds(core * rows, rows)
     swaps[0].wait_recv()
-    swaps[1].wait_recv()
-    pieces = paired(query[mine, :], got_query[...], core)
-    pieces += paired(keyval[0, mine, :], got_keyval[0], core)
+    pieces = paired(keyval[0, mine, :], got_keyval[0], core)
     pieces += paired(keyval[1, mine, :], got_keyval[1], core)
     filled = sum(p.shape[1] for p in pieces)
     pieces.append(jnp.zeros((rows, mixed - filled), F32))
-    my_qkv[...] = jnp.concatenate(pieces, axis=1).astype(BF16)
+    my_keyval[...] = jnp.concatenate(pieces, axis=1).astype(BF16)
     spread.begin(0)
+    swaps[1].wait_recv()
+    my_query[...] = jnp.concatenate(
+        paired(query[mine, :], got_query[...], core), axis=1
+    ).astype(BF16)
+    spread.begin(1)
     swaps[2].wait_recv()
     my_output[...] = jnp.concatenate(
         paired(output[mine, :], got_output[...], core), axis=1
     ).astype(BF16)
-    spread.begin(1)
     spread.begin(2)
     spread.begin(3)
+    spread.begin(4)
     swaps[3].wait_recv()
     my_down[...] = jnp.concatenate(
         paired(down[pl.ds(core * deep, deep), :], got_down[...], core), axis=1
     ).astype(BF16)
-    spread.begin(4)
+    spread.begin(5)
     own = [
         pltpu.make_async_copy(
             sources[part],
             target(part, spread.z, spread.x, spread.y, core),
             local.at[part],
         )
-        for part in range(5)
+        for part in range(6)
     ]
     for copy in own:
         copy.start()
-    spread.all_steps(range(5))
+    spread.all_steps(range(6))
     for copy in own:
         copy.wait()
     for swap in swaps:
         swap.wait_send()
+    pairs[...] = in_pairs(all_keyval[...].astype(F32)).astype(BF16)
+    last = pltpu.make_async_copy(
+        pairs, w_qkv.at[:, pl.ds(width, pairs.shape[1])], local.at[6]
+    )
+    last.start()
+    last.wait()
 
 
 def gather_weights(query, keyval, output, gateup, down):
@@ -706,14 +735,15 @@
     deep = down.shape[0]
     blks, heads = lax.axis_size("blk"), lax.axis_size("head")
     narrow = keyval.shape[2]
-    mixed = -(-2 * (wide + 2 * narrow) // TILE) * TILE
+    mixed = -(-4 * narrow // TILE) * TILE
+    double = heads * narrow * 2
     dma = pltpu.SemaphoreType.DMA
     vmem = pl.BlockSpec(memory_space=pltpu.VMEM)
     shape = jax.ShapeDtypeStruct
     return pl.pallas_call(
         functools.partial(gather_kernel, blks // 2),
         out_shape=[
-            shape((blks * rows, heads // 2 * mixed), BF16),
+            shape((blks * rows, heads * wide + double), BF16),
             shape((blks * rows, heads * wide), BF16),
             shape((2, blks * rows, heads * gateup.shape[2]), BF16),
             shape((blks * deep, heads * wide), BF16),
@@ -725,16 +755,19 @@
             pltpu.VMEM((2, rows // 2, narrow), BF16),
             pltpu.VMEM((rows // 2, wide), BF16),
             pltpu.VMEM((deep // 2, wide), BF16),
+            pltpu.VMEM((rows // 2, 2 * wide), BF16),
             pltpu.VMEM((rows // 2, mixed), BF16),
             pltpu.VMEM((rows // 2, 2 * wide), BF16),
             pltpu.VMEM((deep // 2, 2 * wide), BF16),
+            pltpu.VMEM((blks * rows, heads // 2 * mixed), BF16),
+            pltpu.VMEM((blks * rows, double), BF16),
             dma((4,)),
             dma((4,)),
-            dma((5,)),
-            *Spread.semaphores(5, blks // 2),
+            dma((7,)),
+            *Spread.semaphores(6, blks // 2),
         ],
         compiler_params=pltpu.CompilerParams(
-            collective_id=0, has_side_effects=True, vmem_limit_bytes=24 << 20
+            collective_id=0, has_side_effects=True, vmem_limit_bytes=40 << 20
         ),
     )(query, keyval, output, gateup, down)
 
@@ -782,11 +815,12 @@
     return jnp.concatenate([bias, bias], axis=1)
 
 
-def each_block(blocks, body):
+def each_block(blocks, body, between=lambda: None):
     span = 4 * HEAD_DIM
     fixed, reach, offset = windows(blocks, span, lax.axis_index("head"))
     for block, (start, count) in enumerate(fixed):
         body(block, start, count)
+        between()
 
     @pl.loop(len(fixed), blocks)
     def _(block):
@@ -843,67 +877,515 @@
     )(limits, queries, pairs)
 
 
+def meet(others):
+    barrier = pltpu.get_barrier_semaphore()
+    for other in others:
+        pl.semaphore_signal(barrier, inc=1, device_id=other, device_id_type=MESH)
+    pl.semaphore_wait(barrier, len(others))
+
+
+def remote(source, target, out, into, other):
+    return pltpu.make_async_remote_copy(
+        src_ref=source,
+        dst_ref=target,
+        send_sem=out,
+        recv_sem=into,
+        device_id=other,
+        device_id_type=MESH,
+    )
+
+
+def along(count):
+    blk, head = lax.axis_index("blk"), lax.axis_index("head")
+    return [((blk + ahead) % count, head) for ahead in range(1, count)]
+
+
+def beside():
+    z, x, y, core = place()
+    return [
+        device(z, x, y, 1 - core),
+        device(z, x, 1 - y, core),
+        device(z, x, 1 - y, 1 - core),
+    ]
+
+
+class Exchange:
+    def __init__(self, source, target, size, out, into, local):
+        count = target.shape[0]
+        blk, head = lax.axis_index("blk"), lax.axis_index("head")
+        self.own = pltpu.make_async_copy(source.at[pl.ds(blk * size, size)], target.at[blk], local)
+        self.copies, self.arrivals = [], []
+        for at, (other, _) in enumerate(along(count)):
+            self.copies.append(
+                remote(
+                    source.at[pl.ds(other * size, size)],
+                    target.at[blk],
+                    out.at[at],
+                    into.at[at],
+                    (other, head),
+                )
+            )
+            giver = (blk + count - 1 - at) % count
+            self.arrivals.append(
+                remote(target.at[giver], target.at[giver], out.at[at], into.at[at], (other, head))
+            )
+
+    def start(self):
+        self.own.start()
+        for copy in self.copies:
+            copy.start()
+
+    def wait(self):
+        for copy in self.arrivals:
+            copy.wait_recv()
+        for copy in self.copies:
+            copy.wait_send()
+        self.own.wait()
+
+
+class Quarters:
+    def __init__(self, terms, low, got, out, into):
+        z, x, y, core = place()
+        self.size = low.shape[1] // 4
+        self.terms, self.low, self.got = terms, low, got
+        self.mine = pl.ds((y * 2 + core) * self.size, self.size)
+        self.copies = []
+        for at, (flip_y, flip_core) in enumerate(((0, 1), (1, 0), (1, 1))):
+            other_y, other_core = (y + flip_y) % 2, (core + flip_core) % 2
+            theirs = pl.ds((other_y * 2 + other_core) * self.size, self.size)
+            self.copies.append(
+                remote(
+                    low.at[:, theirs],
+                    got.at[at],
+                    out.at[at],
+                    into.at[at],
+                    device(z, x, other_y, other_core),
+                )
+            )
+
+    def start(self):
+        self.low[...] = self.terms[...].astype(BF16)
+        for copy in self.copies:
+            copy.start()
+
+    def total(self):
+        for copy in self.copies:
+            copy.wait_recv()
+        total = self.terms[:, self.mine]
+        for at in range(3):
+            total = total + self.got[at].astype(F32)
+        return total.astype(BF16)
+
+    def end(self):
+        for copy in self.copies:
+            copy.wait_send()
+
+
+def turned(tile, cosine, sine, only_low=False):
+    lane = lax.broadcasted_iota(jnp.int32, tile.shape, 1)
+    half = HEAD_DIM // 2
+    partner = jnp.where(
+        lane % HEAD_DIM < half, pltpu.roll(tile, TILE - half, 1), pltpu.roll(tile, half, 1)
+    )
+    result = tile * cosine + partner * sine
+    return jnp.where(lane < HEAD_DIM, result, tile) if only_low else result
+
+
 def attend_back_kernel(
-    limits_ref, q_ref, kv_ref, lse_ref, grad_ref, dq_ref, dkv_ref, q_rows, g_rows, kv_turned, total
+    lines,
+    limits_ref,
+    q_ref,
+    kv_ref,
+    lse_ref,
+    grad_ref,
+    turn_ref,
+    output_ref,
+    terms_ref,
+    dqkv_ref,
+    moved_ref,
+    shared_ref,
+    q_rows,
+    g_rows,
+    kv_turned,
+    total,
+    pair_low,
+    pair_got,
+    kept,
+    y_low,
+    y_got,
+    low,
+    got,
+    shard,
+    pair_out,
+    pair_in,
+    y_out,
+    y_in,
+    move_out,
+    move_in,
+    four_out,
+    four_in,
+    local,
+    *sems,
 ):
     blocks, span = q_rows.shape[0], q_rows.shape[2]
+    width = q_ref.shape[1]
+    groups = width // (2 * TILE)
     scale = HEAD_DIM**-0.5
-    for slot, tile in enumerate(tiles_of(q_ref, False)):
-        q_rows[:, slot] = (tile * BF16(scale)).reshape(blocks, span, TILE)
-    for slot, tile in enumerate(tiles_of(grad_ref, True)):
-        g_rows[:, slot] = tile.reshape(blocks, span, TILE)
-    kv_turned[...] = kv_ref[...].astype(F32).T.astype(BF16)
-    total[...] = jnp.zeros_like(total)
-
-    def body(block, start, count):
-        keys = pl.ds(start, count)
-        queries = q_rows[block].reshape(4 * span, TILE)
-        grads = g_rows[block].reshape(4 * span, TILE)
-        scores = dot(kv_ref[keys, :], queries, 1, 1)
-        scores = scores + bias_of(limits_ref, block, start, count)
-        probs = jnp.exp(scores - lse_ref[0, pl.ds(block, 1), :])
-        grad_probs = dot(kv_ref[keys, :], grads, 1, 1)
-        inner = jnp.sum(probs * grad_probs, axis=0, keepdims=True)
-        grad_scores = (probs * (grad_probs - inner)).astype(BF16)
-        total[keys, :] += dot(grad_scores, queries) + dot(probs.astype(BF16), grads)
-        grad_q = (dot(kv_turned[:, keys], grad_scores) * scale).T
-        for at, tile in enumerate(joined(grad_q, False)):
-            dq_ref[pl.ds(block * span, span), at * TILE : (at + 1) * TILE] = tile
-
-    each_block(blocks, body)
-    dkv_ref[...] = total[...]
-
-
-def attend_back(limits, queries, pairs, lse, grads):
+    z, x, y, core = place()
+    size = shard.shape[1]
+
+    def target(part, z, x, y, core):
+        return shared_ref.at[z * 2 + x, :, pl.ds((y * 2 + core) * size, size)]
+
+    spread = Spread([shard], target, lines, sems)
+    meet(along(blocks) + beside())
+    exchange = Exchange(output_ref, moved_ref, span, move_out, move_in, local.at[0])
+    exchange.start()
+    quarters = Quarters(terms_ref, low, got, four_out, four_in)
+    quarters.start()
+    own = pltpu.make_async_copy(shard, target(0, z, x, y, core), local.at[1])
+
+    def gather_start():
+        shard[...] = quarters.total()
+        own.start()
+        spread.begin(0)
+
+    def line(distance):
+        def run():
+            spread.line_step(0, distance, 1)
+            spread.line_step(0, distance, -1)
+
+        return run
+
+    def planes(first):
+        def run():
+            spread.plane_step(0, first)
+            spread.plane_step(0, first + 1)
+
+        return run
+
+    def corners(first):
+        def run():
+            spread.corner_step(0, first)
+            spread.corner_step(0, first + 1)
+
+        return run
+
+    later = [None, None, None, gather_start, None]
+    later += [line(1), None, line(2), None, line(3), None, planes(0), None, planes(2), None]
+    later += [corners(0), None, corners(2)]
+
+    def pump():
+        if later:
+            step = later.pop(0)
+            if step is not None:
+                step()
+
+    def pair_copy(m):
+        return remote(
+            pair_low.at[m, 1 - core],
+            pair_got.at[m],
+            pair_out.at[m],
+            pair_in.at[m],
+            device(z, x, y, 1 - core),
+        )
+
+    def y_copy(m):
+        return remote(
+            y_low.at[m], y_got.at[m], y_out.at[m], y_in.at[m], device(z, x, 1 - y, core)
+        )
+
+    def give(m):
+        whole = total[...].reshape(blocks, 4, span, TILE)
+        for at in range(4):
+            pair_low[m, at % 2, at // 2] = whole[:, at].astype(BF16)
+        spot = total.reshape(blocks, 4, span, TILE)
+        for at in range(2):
+            kept[m, at] = spot[:, at * 2 + core]
+        pair_copy(m).start()
+
+    def add_pair(m):
+        pair_copy(m).wait_recv()
+        y_low[m] = (kept[m, 1 - y] + pair_got[m, 1 - y].astype(F32)).astype(BF16)
+        y_copy(m).start()
+
+    def add_y(m):
+        y_copy(m).wait_recv()
+        tile = kept[m, y] + pair_got[m, y].astype(F32) + y_got[m].astype(F32)
+        tile = turned(tile.reshape(blocks * span, TILE), turn_ref[0], -turn_ref[1], True)
+        at = width + m * TILE
+        dqkv_ref[:, at : at + TILE] = tile.astype(BF16)
+
+    for m in range(groups):
+        columns = slice(m * 2 * TILE, (m + 1) * 2 * TILE)
+        tile = slice(m * TILE, (m + 1) * TILE)
+        for slot, rows in enumerate(tiles_of(q_ref[:, columns], False)):
+            q_rows[:, slot] = (rows * BF16(scale)).reshape(blocks, span, TILE)
+        for slot, rows in enumerate(tiles_of(grad_ref[:, columns], True)):
+            g_rows[:, slot] = rows.reshape(blocks, span, TILE)
+        kv_turned[...] = kv_ref[:, tile].astype(F32).T.astype(BF16)
+        total[...] = jnp.zeros_like(total)
+
+        def body(block, start, count):
+            keys = pl.ds(start, count)
+            queries = q_rows[block].reshape(4 * span, TILE)
+            grads = g_rows[block].reshape(4 * span, TILE)
+            scores = dot(kv_ref[keys, tile], queries, 1, 1)
+            scores = scores + bias_of(limits_ref, block, start, count)
+            probs = jnp.exp(scores - lse_ref[m, pl.ds(block, 1), :])
+            grad_probs = dot(kv_ref[keys, tile], grads, 1, 1)
+            inner = jnp.sum(probs * grad_probs, axis=0, keepdims=True)
+            grad_scores = (probs * (grad_probs - inner)).astype(BF16)
+            total[keys, :] += dot(grad_scores, queries) + dot(probs.astype(BF16), grads)
+            grad_q = (dot(kv_turned[:, keys], grad_scores) * scale).T
+            rows = pl.ds(block * span, span)
+            cosine, sine = turn_ref[0, rows, :], -turn_ref[1, rows, :]
+            for at, part in enumerate(joined(grad_q, False)):
+                at = m * 2 * TILE + at * TILE
+                dqkv_ref[rows, at : at + TILE] = turned(part, cosine, sine).astype(BF16)
+
+        each_block(blocks, body, pump)
+        give(m)
+        if m >= 1:
+            add_pair(m - 1)
+        if m >= 2:
+            add_y(m - 2)
+    while later:
+        pump()
+    add_pair(groups - 1)
+    add_y(groups - 2)
+    for z_at in range(lines):
+        spread.end(0, z_at)
+    own.wait()
+    exchange.wait()
+    quarters.end()
+    add_y(groups - 1)
+    for m in range(groups):
+        pair_copy(m).wait_send()
+        y_copy(m).wait_send()
+
+
+def attend_back(limits, queries, pairs, lse, grads, turn, output, terms):
     rows, width = queries.shape
     blocks = limits.shape[1]
+    span = rows // blocks
     groups = width // (2 * TILE)
-    wide = pl.BlockSpec((rows, 2 * TILE), lambda m: (0, m))
-    long = pl.BlockSpec((pairs.shape[0], TILE), lambda m: (0, m))
-    each = pltpu.VMEM((blocks, 4, rows // blocks, TILE), BF16)
+    rank, total = terms.shape
+    seqs = lax.axis_size("blk")
+    each = pltpu.VMEM((blocks, 4, span, TILE), BF16)
+    dma = pltpu.SemaphoreType.DMA
+    vmem = pl.BlockSpec(memory_space=pltpu.VMEM)
+    shape = jax.ShapeDtypeStruct
     return pl.pallas_call(
-        attend_back_kernel,
-        grid=(groups,),
+        functools.partial(attend_back_kernel, seqs // 2),
         out_shape=[
-            jax.ShapeDtypeStruct((rows, width), F32),
-            jax.ShapeDtypeStruct(pairs.shape, F32),
+            shape((rows, width + pairs.shape[1]), BF16),
+            shape((seqs, span, width), BF16),
+            shape((seqs, rank, total), BF16),
         ],
-        in_specs=[
-            pl.BlockSpec(limits.shape, lambda m: (0, 0, 0)),
-            wide,
-            long,
-            pl.BlockSpec((1, blocks, 2 * TILE), lambda m: (m, 0, 0)),
-            wide,
-        ],
-        out_specs=[wide, long],
+        in_specs=[vmem] * 8,
+        out_specs=[vmem, ANYWHERE, ANYWHERE],
         scratch_shapes=[
             each,
             each,
             pltpu.VMEM((TILE, pairs.shape[0]), BF16),
             pltpu.VMEM((pairs.shape[0], TILE), F32),
+            pltpu.VMEM((groups, 2, 2, blocks, span, TILE), BF16),
+            pltpu.VMEM((groups, 2, blocks, span, TILE), BF16),
+            pltpu.VMEM((groups, 2, blocks, span, TILE), F32),
+            pltpu.VMEM((groups, blocks, span, TILE), BF16),
+            pltpu.VMEM((groups, blocks, span, TILE), BF16),
+            pltpu.VMEM((rank, total), BF16),
+            pltpu.VMEM((3, rank, total // 4), BF16),
+            pltpu.VMEM((rank, total // 4), BF16),
+            dma((groups,)),
+            dma((groups,)),
+            dma((groups,)),
+            dma((groups,)),
+            dma((seqs - 1,)),
+            dma((seqs - 1,)),
+            dma((3,)),
+            dma((3,)),
+            dma((2,)),
+            *Spread.semaphores(1, seqs // 2),
         ],
-        compiler_params=pltpu.CompilerParams(vmem_limit_bytes=48 << 20),
-    )(limits, queries, pairs, lse, grads)
+        compiler_params=pltpu.CompilerParams(
+            collective_id=1, has_side_effects=True, vmem_limit_bytes=56 << 20
+        ),
+    )(limits, queries, pairs, lse, grads, turn, output, terms)
+
+
+def first_back_kernel(
+    lines,
+    dqkv_ref,
+    weight_ref,
+    down_ref,
+    up_ref,
+    normed_ref,
+    low_ref,
+    middle_ref,
+    flat_ref,
+    inverse_ref,
+    gain_ref,
+    moved_ref,
+    shared_ref,
+    result,
+    terms,
+    low,
+    got,
+    shard,
+    move_out,
+    move_in,
+    four_out,
+    four_in,
+    local,
+    *sems,
+):
+    blocks, span = moved_ref.shape[:2]
+    z, x, y, core = place()
+    size = shard.shape[1]
+    rank = down_ref.shape[0] // 3
+    width = flat_ref.shape[1]
+
+    def target(part, z, x, y, core):
+        return shared_ref.at[z * 2 + x, :, pl.ds((y * 2 + core) * size, size)]
+
+    spread = Spread([shard], target, lines, sems)
+    meet(along(blocks) + beside())
+    grad_low = (ADAPTER_SCALE * dot(dqkv_ref[...], up_ref[...], 1, 1)).astype(BF16)
+    grad = dot(dqkv_ref[...], weight_ref[...], 1, 1) + dot(grad_low, down_ref[...])
+    weighted = grad * gain_ref[...]
+    flat, inverse = flat_ref[...].astype(F32), inverse_ref[...]
+    mean = jnp.mean(flat * weighted, axis=1, keepdims=True)
+    grad = middle_ref[...] + inverse * weighted - flat * (inverse * inverse * inverse * mean)
+    result[...] = grad.astype(BF16)
+    exchange = Exchange(result, moved_ref, span, move_out, move_in, local.at[0])
+    exchange.start()
+    grad_up = ADAPTER_SCALE * dot(low_ref[...], dqkv_ref[...], 0, 0)
+    grad_down = dot(grad_low, normed_ref[...], 0, 0)
+    terms[:, :width] = grad_up[:rank, :width]
+    at = width
+    while at < dqkv_ref.shape[1]:
+        lane = lax.broadcasted_iota(jnp.int32, (rank, TILE), 1)
+        terms[:, at : at + TILE] = jnp.where(
+            lane < HEAD_DIM,
+            grad_up[rank : 2 * rank, at : at + TILE],
+            grad_up[2 * rank :, at : at + TILE],
+        )
+        at += TILE
+    for which in range(3):
+        terms[:, at : at + width] = grad_down[which * rank : (which + 1) * rank]
+        at += width
+    if at < terms.shape[1]:
+        terms[:, at:] = jnp.zeros((rank, terms.shape[1] - at), F32)
+    quarters = Quarters(terms, low, got, four_out, four_in)
+    quarters.start()
+    shard[...] = quarters.total()
+    own = pltpu.make_async_copy(shard, target(0, z, x, y, core), local.at[1])
+    own.start()
+    spread.begin(0)
+    spread.all_steps([0])
+    own.wait()
+    quarters.end()
+    exchange.wait()
+
+
+def first_back(grad_qkv, weight, down, up, normed, low, middle, flat, inverse, gain):
+    rows, width = flat.shape
+    rank = down.shape[0] // 3
+    seqs, heads = lax.axis_size("blk"), lax.axis_size("head")
+    total = 3 * width + weight.shape[1]
+    total += -total % (2 * heads * TILE)
+    dma = pltpu.SemaphoreType.DMA
+    vmem = pl.BlockSpec(memory_space=pltpu.VMEM)
+    shape = jax.ShapeDtypeStruct
+    return pl.pallas_call(
+        functools.partial(first_back_kernel, seqs // 2),
+        out_shape=[
+            shape((seqs, rows // seqs, width), BF16),
+            shape((seqs, rank, total), BF16),
+        ],
+        in_specs=[vmem] * 10,
+        out_specs=[ANYWHERE, ANYWHERE],
+        scratch_shapes=[
+            pltpu.VMEM((rows, width), BF16),
+            pltpu.VMEM((rank, total), F32),
+            pltpu.VMEM((rank, total), BF16),
+            pltpu.VMEM((3, rank, total // 4), BF16),
+            pltpu.VMEM((rank, total // 4), BF16),
+            dma((seqs - 1,)),
+            dma((seqs - 1,)),
+            dma((3,)),
+            dma((3,)),
+            dma((2,)),
+            *Spread.semaphores(1, seqs // 2),
+        ],
+        compiler_params=pltpu.CompilerParams(
+            collective_id=2, has_side_effects=True, vmem_limit_bytes=56 << 20
+        ),
+    )(grad_qkv, weight, down, up, normed, low, middle, flat, inverse, gain.reshape(1, -1))
+
+
+def placed_kernel(sizes, width, holder_ref, early_ref, late_ref, *outs):
+    q_down, q_up, kv_down, kv_up, o_down, o_up, gu_down, gu_up, ff_down, ff_up = outs
+    cuts = np.cumsum([0] + sizes)
+    early = [slice(int(begin), int(end)) for begin, end in zip(cuts[:-1], cuts[1:])]
+    for out, cut in zip((o_down, o_up), early[:2]):
+        out[0] = early_ref[0, :, cut].astype(F32)
+    for which in range(2):
+        gu_down[0, which] = early_ref[0, :, early[2 + which]].astype(F32)
+        gu_up[0, which] = early_ref[0, :, early[4 + which]].astype(F32)
+    for out, cut in zip((ff_down, ff_up), early[6:]):
+        out[0] = early_ref[0, :, cut].astype(F32)
+    q_up[0] = late_ref[0, :, :width].astype(F32)
+    narrow = KV_HEADS * HEAD_DIM
+    pairs = late_ref[0, :, width : width + 2 * narrow].astype(F32)
+    for which in range(2):
+        pieces = [
+            pairs[:, (2 * head + which) * HEAD_DIM : (2 * head + which + 1) * HEAD_DIM]
+            for head in range(KV_HEADS)
+        ]
+        kv_up[0, which] = jnp.concatenate(pieces, axis=1)
+    at = width + 2 * narrow
+    q_down[0] = late_ref[0, :, at : at + width].astype(F32)
+    for which in range(2):
+        at += width
+        kv_down[0, which] = late_ref[0, :, at : at + width].astype(F32)
+
+
+def placed(holder, early, late, sizes, width):
+    adapters, rank = early.shape[:2]
+    hidden = sizes[4]
+    narrow = KV_HEADS * HEAD_DIM
+    shapes = [
+        (rank, width),
+        (rank, width),
+        (2, rank, width),
+        (2, rank, narrow),
+        (rank, width),
+        (rank, width),
+        (2, rank, width),
+        (2, rank, hidden),
+        (rank, hidden),
+        (rank, width),
+    ]
+
+    def whole(shape):
+        return pl.BlockSpec((1,) + shape, lambda a, held: (a,) + (0,) * len(shape))
+
+    return pl.pallas_call(
+        functools.partial(placed_kernel, sizes, width),
+        grid_spec=pltpu.PrefetchScalarGridSpec(
+            num_scalar_prefetch=1,
+            grid=(adapters,),
+            in_specs=[
+                pl.BlockSpec((1, rank, early.shape[2]), lambda a, held: (held[a], 0, 0)),
+                pl.BlockSpec((1, rank, late.shape[2]), lambda a, held: (held[a], 0, 0)),
+            ],
+            out_specs=[whole(shape) for shape in shapes],
+        ),
+        out_shape=[jax.ShapeDtypeStruct((adapters,) + shape, F32) for shape in shapes],
+    )(holder, early, late)
 
 
 def by_sequence(
@@ -954,36 +1436,17 @@
     u_gateup, u_ffdown = gateup_up[adapter], ffdown_up[adapter]
     rank = d_query.shape[0]
 
-    half, narrow = width // 2, u_keyval.shape[2] // 2
-    mixed = w_qkv.shape[1] // 2
-    fill = mixed - half - 2 * narrow
-
-    def interleaved(query, key, value):
-        empty = jnp.zeros(query.shape[:-1] + (fill,), query.dtype)
-        pieces = []
-        for y in (0, 1):
-            pieces += [
-                query[:, y * half : (y + 1) * half],
-                key[:, y * narrow : (y + 1) * narrow],
-                value[:, y * narrow : (y + 1) * narrow],
-                empty,
-            ]
-        return jnp.concatenate(pieces, axis=1)
-
-    def separated(array):
-        def at(begin, size):
-            return jnp.concatenate(
-                [array[:, y * mixed + begin : y * mixed + begin + size] for y in (0, 1)], axis=1
-            )
-
-        return at(0, half), at(half, narrow), at(half + narrow, narrow)
-
-    nil_q, nil_k = jnp.zeros_like(u_query), jnp.zeros_like(u_keyval[0])
+    def in_turn(first, second):
+        cut = (first.shape[0], KV_HEADS, HEAD_DIM)
+        both = jnp.concatenate([first.reshape(cut), second.reshape(cut)], axis=2)
+        return both.reshape(first.shape[0], 2 * first.shape[1])
+
+    nil = jnp.zeros_like(u_keyval[0])
+    u_keys, u_values = in_turn(u_keyval[0], nil), in_turn(nil, u_keyval[1])
     u_qkv = jnp.concatenate(
         [
-            interleaved(u_query, nil_k, nil_k),
-            interleaved(nil_q, u_keyval[0], nil_k),
-            interleaved(nil_q, nil_k, u_keyval[1]),
+            jnp.pad(u_query, ((0, 0), (0, u_keys.shape[1]))),
+            jnp.pad(jnp.concatenate([u_keys, u_values], axis=0), ((0, 0), (width, 0))),
         ],
         axis=0,
     )
@@ -1022,16 +1485,26 @@
     limits = jnp.stack([least, most, position])
     limits = jnp.concatenate([limits, limits], axis=2)
 
+    flat_pos = position.reshape(rows)
+    freqs = ROPE_BASE ** (
+        -(jnp.arange(HEAD_DIM // 2, dtype=F32) * 2.0) / HEAD_DIM
+    )
+    angles = flat_pos.astype(F32)[:, None] * freqs[None, :]
+    cosine, sine = jnp.cos(angles), jnp.sin(angles)
+    turn = jnp.stack(
+        [jnp.tile(cosine, (1, 4)), jnp.tile(jnp.concatenate([-sine, sine], axis=1), (1, 2))]
+    )
+
     normed, inverse1 = norm(flat, attn_gain)
     qkv, low_qkv = project(normed, w_qkv, d_qkv, u_qkv)
-    queries, keys, values = separated(qkv)
-    flat_pos = position.reshape(rows)
+    queries, pairs = qkv[:, :width], qkv[:, width:]
     heads, kv_heads = HEADS, KV_HEADS
     queries = rotate(queries.reshape(rows, heads, HEAD_DIM), flat_pos, 1.0)
     queries = queries.astype(BF16).reshape(rows, width)
-    keys = rotate(keys.reshape(rows, kv_heads, HEAD_DIM), flat_pos, 1.0).astype(BF16)
-    values = values.reshape(rows, kv_heads, HEAD_DIM).astype(BF16)
-    pairs = jnp.concatenate([keys, values], axis=2).reshape(seqs, part, 2 * kv_heads * HEAD_DIM)
+    pairs = pairs.reshape(rows, kv_heads, 2 * HEAD_DIM)
+    keys = rotate(pairs[:, :, :HEAD_DIM], flat_pos, 1.0)
+    pairs = jnp.concatenate([keys, pairs[:, :, HEAD_DIM:]], axis=2).astype(BF16)
+    pairs = pairs.reshape(seqs, part, 2 * kv_heads * HEAD_DIM)
     pairs = lax.all_gather(pairs, "head", axis=1, tiled=True)
     pairs = pairs.reshape(seqs * span, 2 * kv_heads * HEAD_DIM)
     attended, lse = attend(limits, queries, pairs)
@@ -1064,67 +1537,32 @@
     grad_mixed, gd_output, gu_output = project_back(
         attended, low_output, grad_middle.astype(BF16), w_output, d_output, u_output
     )
-    grad_query, grad_pairs = attend_back(limits, queries, pairs, lse, grad_mixed.astype(BF16))
-    grad_pairs = lax.psum_scatter(
-        grad_pairs.reshape(seqs, span, -1), "head", scatter_dimension=1, tiled=True
-    ).reshape(rows, kv_heads, 2 * HEAD_DIM)
-    grad_query = rotate(grad_query.reshape(rows, heads, HEAD_DIM), flat_pos, -1.0)
-    grad_keys = rotate(grad_pairs[:, :, :HEAD_DIM], flat_pos, -1.0)
-    grad_values = grad_pairs[:, :, HEAD_DIM:]
-    grad_qkv = interleaved(
-        grad_query.astype(BF16).reshape(rows, width),
-        grad_keys.astype(BF16).reshape(rows, kv_heads * HEAD_DIM),
-        grad_values.astype(BF16).reshape(rows, kv_heads * HEAD_DIM),
-    )
-    grad_normed, gd_qkv, gu_qkv = project_back(normed, low_qkv, grad_qkv, w_qkv, d_qkv, u_qkv)
-    input_grad = grad_middle + norm_back(flat, inverse1, attn_gain, grad_normed)
-
-    gu_query = separated(gu_qkv[:rank])[0]
-    gu_key = separated(gu_qkv[rank : 2 * rank])[1]
-    gu_value = separated(gu_qkv[2 * rank :])[2]
-    terms = [
-        gd_qkv[:rank],
-        gu_query,
-        gd_qkv[rank : 2 * rank],
-        gd_qkv[2 * rank :],
-        gu_key,
-        gu_value,
-        gd_output,
-        gu_output,
-        gd_gate,
-        gd_up,
-        gu_gate,
-        gu_up,
-        gd_ffdown,
-        gu_ffdown,
-    ]
-    sizes = [term.shape[1] for term in terms]
-    unit = groups * TILE
-    extra = -sum(sizes) % unit
-    terms.append(jnp.zeros((rank, extra), F32))
-    shared = lax.psum_scatter(
-        jnp.concatenate(terms, axis=1), "head", scatter_dimension=1, tiled=True
-    )
-    shared = lax.all_gather(shared.astype(BF16), ("blk", "head"), axis=0)
-    shared = shared.reshape(seqs, groups, rank, -1).swapaxes(1, 2).reshape(seqs, rank, -1)
+    early = [gd_output, gu_output, gd_gate, gd_up, gu_gate, gu_up, gd_ffdown, gu_ffdown]
+    sizes = [term.shape[1] for term in early]
+    fill = -sum(sizes) % (2 * groups * TILE)
+    early = jnp.concatenate(early + [jnp.zeros((rank, fill), F32)], axis=1)
+    grad_qkv, output, early = attend_back(
+        limits, queries, pairs, lse, grad_mixed.astype(BF16), turn, output, early
+    )
+    input_grad, late = first_back(
+        grad_qkv, w_qkv, d_qkv, u_qkv, normed, low_qkv, grad_middle, flat, inverse1, attn_gain
+    )
     adapters = jnp.arange(query_down.shape[0], dtype=jnp.int32)
-    holder = jnp.argmax(adapter_index[None, :] == adapters[:, None], axis=1)
-    shared = shared[holder]
-    cuts = np.cumsum([0] + sizes)
-    found = [shared[:, :, begin:end].astype(F32) for begin, end in zip(cuts[:-1], cuts[1:])]
+    holder = jnp.argmax(adapter_index[None, :] == adapters[:, None], axis=1).astype(jnp.int32)
+    found = placed(holder, early, late, sizes, width)
     return (
-        moved(output.reshape(seqs, part, width)),
-        moved(input_grad.astype(BF16).reshape(seqs, part, width)),
+        output,
+        input_grad,
         found[0].swapaxes(1, 2),
         found[1],
-        jnp.stack([found[2], found[3]], axis=1).swapaxes(2, 3),
-        jnp.stack([found[4], found[5]], axis=1),
-        found[6].swapaxes(1, 2),
+        found[2].swapaxes(2, 3),
+        found[3],
+        found[4].swapaxes(1, 2),
+        found[5],
+        found[6].swapaxes(2, 3),
         found[7],
-        jnp.stack([found[8], found[9]], axis=1).swapaxes(2, 3),
-        jnp.stack([found[10], found[11]], axis=1),
-        found[12].swapaxes(1, 2),
-        found[13],
+        found[8].swapaxes(1, 2),
+        found[9],
     )
 
 

time: 700 us -> 596 us (0.85)
  Pallas kernels: 246 us -> 366 us
  waiting for transfers between devices: 88.3 us -> 0.02 us
  local copies, waits for them, and re-layouts: 100 us -> 43 us
  blocking collectives: 50.4 us -> 0 us
  matrix products: 137 us -> 127 us
  other arithmetic: 31.2 us -> 22.1 us
    pallas_call x1 -> x3, Pallas kernels: 41.3 us -> 160 us  [the longest x1 87.4 us: attend_back(): pl.pallas_call(functools.partial(attend_back_kernel, seqs // 2), out_shap...]
    reduce_scatter x2 -> x0, waiting for transfers between devices: 59.2 us -> none  [the longest x1 31.6 us: by_sequence(): lax.psum_scatter(grad_pairs.reshape(seqs, span, -1), 'head', scatter_dime...]
    all_to_all x1 -> x0, blocking collectives: 50.4 us -> none  [moved(): return lax.all_to_all(array, 'blk', split_axis=0, concat_axis=0, tiled=True)]
    all_to_all x3 -> x2, waiting for transfers between devices: 29.1 us -> 0.01 us  [moved(): return lax.all_to_all(array, 'blk', split_axis=0, concat_axis=0, tiled=True)]
    unnamed x154 -> x121, local copies, waits for them, and re-layouts: 37.1 us -> 16.5 us
    reshape x4 -> x1, local copies, waits for them, and re-layouts: 20.5 us -> 0.78 us  [in_turn(): return both.reshape(first.shape[0], 2 * first.shape[1])]
    dot_general x40 -> x35, matrix products: 137 us -> 127 us  [dot(): lax.dot_general(left, right, (((left_dim,), (right_dim,)), ((), ())), pre...]
    concatenate x9 -> x4, local copies, waits for them, and re-layouts: 9.63 us -> 1.44 us  [the longest x1 0.72 us: by_sequence(): pairs = jnp.concatenate([keys, pairs[:, :, HEAD_DIM:]], axis=2).astype(BF16)]
  transfers between devices with their start and end apart: 7 -> 3, of which waited for: 3 -> 0; matrix products, arithmetic and copies ran while one was open for 14% -> 11% of each run, Pallas kernels for 25% -> 30%
where the time goes in v2:
time: 596 us; the launch traced here: 588 us
  Pallas kernels  366 us (61%)
  matrix products  127 us (21%)
  local copies, waits for them, and re-layouts  43 us (7%)
  other arithmetic  22.1 us (4%)
  between operations  17.8 us (3%)
  starting transfers between devices  12 us (2%)
    pallas_call x1, Pallas kernels, gather_weights(): pl.pallas_call(functools.partial(gather_kernel, blks // 2), out_shape=[sh...  175 us
    dot_general x35, matrix products, dot(): lax.dot_general(left, right, (((left_dim,), (right_dim,)), ((), ())), pre...  127 us
    pallas_call x1, Pallas kernels, attend_back(): pl.pallas_call(functools.partial(attend_back_kernel, seqs // 2), out_shap...  87.4 us
    pallas_call x1, Pallas kernels, first_back(): pl.pallas_call(functools.partial(first_back_kernel, seqs // 2), out_shape...  63 us
    pallas_call x1, Pallas kernels, attend(): pl.pallas_call(attend_kernel, grid=(groups,), out_shape=[jax.ShapeDtypeSt...  31.3 us
    unnamed x121, local copies, waits for them, and re-layouts  16.5 us
  transfers between devices with their start and end apart: 3, of which 0 were waited for; matrix products, arithmetic and copies ran while one was open for 11% of the time, Pallas kernels for 30%

profile of v2, /device:TPU:0, one launch (start us, length us, event | category | flops | bytes accessed | tf_op | source)
XLA Modules:
  0.0 588.0 jit_solution(6263944840561332313)
XLA Ops:
  7.2 7.4 %all-to-all-start = ((bf16[8,64,1280]{2,1,0:T(8,128)(2,1)}), bf16[8,64,1280]{2,1,0:T(8,128)(2,1)}, u32[]{:S(2)}, u32[]{:S(2)}) async-start(bf16[8,64,1280]{2,1,0:T(8,128)(2,1)} %param.22), calls=%async_computation | async-start | bytes 2621440 | tf_op jit(solution)/shard_map/all_to_all | solution.py:1423
  18.2 3.1 gather_fusion
  27.0 175.2 %shard_map.301 = (bf16[1280,1920]{1,0:T(8,128)(2,1)S(1)}, bf16[1280,1280]{1,0:T(8,128)(2,1)S(1)}, bf16[2,1280,3584]{2,1,0:T(8,128)(2,1)}, bf16[3584,1280]{1,0:T(8,128)(2,1)}) custom-call(bf16[160,320]{1,0:T(8,128)(2,1)S(1)} %copy-done.6, bf16[2,160,80]{2,1,0:T(8,128)(2,1)S(1)} %copy-done.9, bf16[160,320]{1,0:T(8,128)(2,1)S(1)} %copy-done.7, ...), custom_call_target="tpu_custom_call" | custom-call | tf_op jit(solution)/shard_map/pallas_call | solution.py:743
  212.6 4.3 all-to-all-start.1
  219.0 3.3 multiply_convert_fusion.4
  222.3 2.9 fusion.87
  241.1 3.5 slice.90
  245.5 3.3 copy.58
  256.1 8.3 %fusion.89 = f32[3584,512]{1,0:T(8,128)S(1)} fusion(bf16[3584,1280]{1,0:T(8,128)(2,1)} %get-tuple-element.38, bf16[512,1280]{1,0:T(8,128)(2,1)} %bitcast.14), kind=kOutput, calls=%fused_computation.161 | convolution fusion | flops 4697620480 | bytes 17825792 | tf_op jit(solution)/shard_map/dot_general | solution.py:411
  264.4 5.0 bitcast_add_fusion
  271.2 31.3 %shard_map.302 = (bf16[512,1280]{1,0:T(8,128)(2,1)S(1)}, f32[5,8,256]{2,1,0:T(8,128)S(1)}) custom-call(s32[3,8,128]{2,1,0:T(8,128)S(1)} %add_add_fusion.limits_ref, bf16[512,1280]{1,0:T(8,128)(2,1)S(1)} %copy.69.q_ref, bf16[2048,640]{1,0:T(8,128)(2,1)S(1)} %bitcast.157), custom_call_target="tpu_custom_call" | custom-call | tf_op jit(solution)/shard_map/pallas_call | solution.py:856
  308.1 23.3 %fusion.2 = f32[512,3584]{0,1:T(8,128)} fusion(bf16[512,1280]{1,0:T(8,128)(2,1)S(1)} %multiply_convert_fusion.3, bf16[2,1280,3584]{2,1,0:T(8,128)(2,1)} %get-tuple-element.39), kind=kOutput, calls=%fused_computation.3 | convolution fusion | flops 4697620480 | bytes 17825792 | tf_op jit(solution)/shard_map/dot_general | solution.py:411
  331.4 12.9 %fusion.6 = f32[512,3584]{0,1:T(8,128)} fusion(bf16[512,1280]{1,0:T(8,128)(2,1)S(1)} %multiply_convert_fusion.3, bf16[2,1280,3584]{2,1,0:T(8,128)(2,1)} %get-tuple-element.39), kind=kOutput, calls=%fused_computation.7 | convolution fusion | flops 4697620480 | bytes 17825792 | tf_op jit(solution)/shard_map/dot_general | solution.py:411
  345.2 7.2 %multiply_add_fusion = f32[512,3584]{0,1:T(8,128)} fusion(f32[512,3584]{0,1:T(8,128)} %fusion.2, bf16[512,16]{0,1:T(8,128)(2,1)S(1)} %convolution_convert_fusion.1, bf16[8,2,16,3584]{3,2,1,0:T(8,128)(2,1)S(1)} %copy-done, s32[]{:T(128)S(6)} %select_n.52), kind=kOutput, calls=%fused_computation.19 | convolution fusion | flops 62390272 | bytes 14811140 | tf_op jit(solution)/shard_map/dot_general | solution.py:411
  352.4 11.4 %multiply_convert_fusion = (bf16[512,3584]{0,1:T(8,128)(2,1)}, bf16[512,3584]{0,1:T(8,128)(2,1)}, bf16[512,3584]{0,1:T(8,128)(2,1)S(1)}) fusion(f32[512,3584]{0,1:T(8,128)} %multiply_add_fusion, f32[512,3584]{0,1:T(8,128)} %bitcast_add_fusion, f32[512,3584]{0,1:T(8,128)} %fusion.6, bf16[512,16]{0,1:T(8,128)(2,1)S(1)} %convolution_convert_fusion.2, ...), kind=kOutput, calls=%fused_computation.14 | convolution fusion | flops 89915392 | bytes 33161224 | tf_op jit(solution)/shard_map/dot_general | solution.py:411
  365.7 9.7 %fusion.15 = f32[512,1280]{1,0:T(8,128)} fusion(f32[512,1280]{1,0:T(8,128)S(1)} %fusion.54, bf16[512,3584]{0,1:T(8,128)(2,1)S(1)} %get-tuple-element.60, bf16[2,1280,3584]{2,1,0:T(8,128)(2,1)} %get-tuple-element.39), kind=kOutput, calls=%fused_computation.28 | convolution fusion | flops 4698275840 | bytes 18087936 | tf_op jit(solution)/shard_map/dot_general | solution.py:411
  375.4 2.6 fusion.37
  379.1 12.0 %multiply_reduce_fusion = (f32[512]{0:T(512)S(1)}, f32[512,1280]{1,0:T(8,128)}) fusion(f32[512,1280]{1,0:T(8,128)S(1)} %get-tuple-element.78, f32[1280]{0:T(1024)} %param.24, f32[512,1280]{1,0:T(8,128)} %fusion.15, f32[512,1280]{1,0:T(8,128)S(1)} %fusion.55, bf16[512,3584]{0,1:T(8,128)(2,1)} %get-tuple-element.59, bf16[2,1280,3584]{2,1,0:T(8,128)(2,1)} %get-tuple-element.39), kind=kOutput, calls=%fused_computation.42 | convolution fusion | flops 4700896768 | bytes 23341056 | tf_op jit(solution)/shard_map/dot_general | solution.py:411
  391.2 2.8 subtract_add_fusion.middle_ref
  398.4 5.2 fusion.90
  405.4 2.4 fusion.31.grad_ref
  418.3 87.4 %shard_map.303 = (bf16[512,1920]{1,0:T(8,128)(2,1)}, bf16[8,64,1280]{2,1,0:T(8,128)(2,1)}, bf16[8,16,17408]{2,1,0:T(8,128)(2,1)}) custom-call(s32[3,8,128]{2,1,0:T(8,128)} %copy-done.8, bf16[512,1280]{1,0:T(8,128)(2,1)} %copy-done.1, bf16[2048,640]{1,0:T(8,128)(2,1)} %bitcast.156, f32[5,8,256]{2,1,0:T(8,128)} %copy-done.10, ...), custom_call_target="tpu_custom_call" | custom-call | tf_op jit(solution)/shard_map/pallas_call | solution.py:1179
  505.7 63.0 %shard_map.304 = (bf16[8,64,1280]{2,1,0:T(8,128)(2,1)}, bf16[8,16,6144]{2,1,0:T(8,128)(2,1)}) custom-call(bf16[512,1920]{1,0:T(8,128)(2,1)} %get-tuple-element.41.dqkv_ref, bf16[1280,1920]{1,0:T(8,128)(2,1)} %copy-done.3, bf16[48,1280]{1,0:T(8,128)(2,1)} %pad_maximum_fusion.4.down_ref, bf16[48,1920]{1,0:T(8,128)(2,1)} %fusion.42.up_ref, ...), custom_call_target="tpu_custom_call" | custom-call | tf_op jit(solution)/shard_map/pallas_call | solution.py:1302
  568.7 9.1 %shard_map.305 = (f32[8,16,1280]{2,1,0:T(8,128)}, f32[8,16,1280]{2,1,0:T(8,128)}, f32[8,2,16,1280]{3,2,1,0:T(8,128)}, f32[8,2,16,320]{3,2,1,0:T(8,128)}, f32[8,1...) custom-call(s32[8]{0:T(128)} %get-tuple-element.43.holder_ref, ...), custom_call_target="tpu_custom_call" | custom-call | tf_op jit(solution)/shard_map/pallas_call | solution.py:1376
  (204 shorter events, 73.6 us)
Async XLA Ops:
  7.2 338.0 %copy-start = (bf16[8,2,16,3584]{3,2,1,0:T(8,128)(2,1)S(1)}, bf16[8,2,16,3584]{3,2,1,0:T(8,128)(2,1)}, u32[]{:S(2)}) copy-start(bf16[8,2,16,3584]{3,2,1,0:T(8,128)(2,1)} %param.37) | copy-start | bytes 5505028
  7.2 205.4 %all-to-all-start = ((bf16[8,64,1280]{2,1,0:T(8,128)(2,1)}), bf16[8,64,1280]{2,1,0:T(8,128)(2,1)}, u32[]{:S(2)}, u32[]{:S(2)}) async-start(bf16[8,64,1280]{2,1,0:T(8,128)(2,1)} %param.22), calls=%async_computation | async-start | bytes 2621440 | tf_op jit(solution)/shard_map/all_to_all | solution.py:1423
  22.9 208.8 %copy-start.26 = (f32[512,32]{0,1:T(8,128)}, f32[512,32]{0,1:T(8,128)S(1)}, u32[]{:S(2)}) copy-start(f32[512,32]{0,1:T(8,128)S(1)} %get-tuple-element.71) | copy-start | bytes 196612
  22.9 208.8 %copy-start.28 = (f32[512,32]{0,1:T(8,128)}, f32[512,32]{0,1:T(8,128)S(1)}, u32[]{:S(2)}) copy-start(f32[512,32]{0,1:T(8,128)S(1)} %get-tuple-element.70) | copy-start | bytes 196612
  23.8 184.9 %copy-start.54 = (s32[8]{0:T(128)S(1)}, s32[8]{0:T(128)}, u32[]{:S(2)}) copy-start(s32[8]{0:T(128)} %copy-done.53) | copy-start | bytes 100
  208.0 10.9 %copy-start.47 = (f32[1280]{0:T(1024)S(1)}, f32[1280]{0:T(1024)}, u32[]{:S(2)}) copy-start(f32[1280]{0:T(1024)} %param.23) | copy-start | bytes 15364
  210.1 15.1 %copy-start.34 = (bf16[16,1280]{1,0:T(8,128)(2,1)}, bf16[16,1280]{1,0:T(8,128)(2,1)S(1)}, u32[]{:S(2)}) copy-start(bf16[16,1280]{1,0:T(8,128)(2,1)S(1)} %dynamic-slice_bitcast_fusion.9) | copy-start | bytes 122884
  210.9 14.8 %copy-start.31 = (bf16[16,1280]{1,0:T(8,128)(2,1)}, bf16[16,1280]{1,0:T(8,128)(2,1)S(1)}, u32[]{:S(2)}) copy-start(bf16[16,1280]{1,0:T(8,128)(2,1)S(1)} %dynamic-slice_bitcast_fusion.8) | copy-start | bytes 122884
  212.6 13.1 %copy-start.24 = (bf16[32,1920]{1,0:T(8,128)(2,1)}, bf16[32,1920]{1,0:T(8,128)(2,1)S(1)}, u32[]{:S(2)}) copy-start(bf16[32,1920]{1,0:T(8,128)(2,1)S(1)} %fusion.43) | copy-start | bytes 368644
  212.6 12.6 %copy-start.35 = (bf16[16,1280]{1,0:T(8,128)(2,1)}, bf16[16,1280]{1,0:T(8,128)(2,1)S(1)}, u32[]{:S(2)}) copy-start(bf16[16,1280]{1,0:T(8,128)(2,1)S(1)} %get-tuple-element.67) | copy-start | bytes 122884
  212.6 12.6 %copy-start.36 = (bf16[16,1280]{1,0:T(8,128)(2,1)}, bf16[16,1280]{1,0:T(8,128)(2,1)S(1)}, u32[]{:S(2)}) copy-start(bf16[16,1280]{1,0:T(8,128)(2,1)S(1)} %get-tuple-element.68) | copy-start | bytes 122884
  212.6 41.2 %all-to-all-start.1 = ((bf16[8,64,1280]{2,1,0:T(8,128)(2,1)}), bf16[8,64,1280]{2,1,0:T(8,128)(2,1)}, u32[]{:S(2)}, u32[]{:S(2)}) async-start(bf16[8,64,1280]{2,1,0:T(8,128)(2,1)} %param.43), calls=%async_computation.1 | async-start | bytes 2621440 | tf_op jit(solution)/shard_map/all_to_all | solution.py:1423
  216.9 52.5 %all-gather.2.cloned.1.call-start = ((), (), s32[]{:S(2)}) async-start(), calls=%async_computation.2 | async-start | bytes 3276800 | tf_op jit(solution)/shard_map/all_gather | solution.py:1508
  236.1 33.3 %copy-start.8 = (s32[3,8,128]{2,1,0:T(8,128)}, s32[3,8,128]{2,1,0:T(8,128)S(1)}, u32[]{:S(2)}) copy-start(s32[3,8,128]{2,1,0:T(8,128)S(1)} %add_add_fusion.limits_ref) | copy-start | bytes 36868
  253.8 15.6 %copy-start.1 = (bf16[512,1280]{1,0:T(8,128)(2,1)}, bf16[512,1280]{1,0:T(8,128)(2,1)S(1)}, u32[]{:S(2)}) copy-start(bf16[512,1280]{1,0:T(8,128)(2,1)S(1)} %copy.69.q_ref) | copy-start | bytes 3932164
  256.1 8.3 %copy-start.41 = (bf16[16,512]{1,0:T(8,128)(2,1)}, bf16[16,512]{1,0:T(8,128)(2,1)S(1)}, u32[]{:S(2)}) copy-start(bf16[16,512]{1,0:T(8,128)(2,1)S(1)} %fusion.35) | copy-start | bytes 49156
  271.2 31.3 %copy-start.12 = (bf16[1280,1280]{1,0:T(8,128)(2,1)S(1)}, bf16[1280,1280]{1,0:T(8,128)(2,1)}, u32[]{:S(2)}) copy-start(bf16[1280,1280]{1,0:T(8,128)(2,1)} %copy-done.11) | copy-start | bytes 9830404
  307.8 23.6 %copy-start.48 = (f32[512]{0:T(512)}, f32[512]{0:T(512)S(1)}, u32[]{:S(2)}) copy-start(f32[512]{0:T(512)S(1)} %add_rsqrt_fusion.1) | copy-start | bytes 6148
  344.8 7.6 %copy-start.43 = (bf16[512,16]{0,1:T(8,128)(2,1)}, bf16[512,16]{0,1:T(8,128)(2,1)S(1)}, u32[]{:S(2)}) copy-start(bf16[512,16]{0,1:T(8,128)(2,1)S(1)} %convolution_convert_fusion.1) | copy-start | bytes 49156
  364.4 11.0 %copy-start.37 = (bf16[512,16]{0,1:T(8,128)(2,1)}, bf16[512,16]{0,1:T(8,128)(2,1)S(1)}, u32[]{:S(2)}) copy-start(bf16[512,16]{0,1:T(8,128)(2,1)S(1)} %fusion.38) | copy-start | bytes 49156
  379.1 12.0 %copy-start.51 = (f32[512]{0:T(512)S(1)}, f32[512]{0:T(512)}, u32[]{:S(2)}) copy-start(f32[512]{0:T(512)} %copy-done.50) | copy-start | bytes 6148
  379.1 12.0 %copy-start.49 = (f32[512]{0:T(512)S(1)}, f32[512]{0:T(512)}, u32[]{:S(2)}) copy-start(f32[512]{0:T(512)} %copy-done.48) | copy-start | bytes 6148
  393.9 13.9 %copy-start.13 = (f32[512,1280]{1,0:T(8,128)}, f32[512,1280]{1,0:T(8,128)S(1)}, u32[]{:S(2)}) copy-start(f32[512,1280]{1,0:T(8,128)S(1)} %subtract_add_fusion.middle_ref) | copy-start | bytes 7864324
  568.7 9.2 %copy-start.21 = (bf16[8,64,1280]{2,1,0:T(8,128)(2,1)S(1)}, bf16[8,64,1280]{2,1,0:T(8,128)(2,1)}, u32[]{:S(2)}) copy-start(bf16[8,64,1280]{2,1,0:T(8,128)(2,1)} %get-tuple-element.97) | copy-start | bytes 3932164
  (38 other events, 132.4 us)
Sparse Core Ops, SparseCore 0:
  235.4 26.9 all-gather.1
